TPU v7x, 512 devices: a whole 4x8x8 slice. The times are simulated.
512 devices in a mesh: heads: 16 (over y, core), seq: 32 (over z, x).
Axes of the slice: x: 4, y: 8, z: 8, core: 2. Of those that a mesh axis runs over, the one named last changes fastest.
Arguments:
- queries: bfloat16 [8192, 4096], P('seq', 'heads'), may hold values from -6 to 6
- keys: bfloat16 [8192, 4096], P('seq', 'heads'), may hold values from -6 to 6
- values: bfloat16 [8192, 4096], P('seq', 'heads'), may hold values from -6 to 6
- src_keys: bfloat16 [4096, 4096], P('seq', 'heads'), may hold values from -6 to 6
- src_values: bfloat16 [4096, 4096], P('seq', 'heads'), may hold values from -6 to 6
- norm_gain: float32 [4096], P('heads'), may hold values from 0.1 to 1.9
- out_weight: bfloat16 [4096, 4096], P('heads'), may hold values from -0.09375 to 0.09375
- grad_out: bfloat16 [8192, 4096], P('seq', 'heads'), may hold values from -6 to 6
Outputs:
- attended: bfloat16 [8192, 4096], P('seq', 'heads')
- grad_queries: bfloat16 [8192, 4096], P('seq', 'heads')
- grad_keys: bfloat16 [8192, 4096], P('seq', 'heads')
- grad_values: bfloat16 [8192, 4096], P('seq', 'heads')
- grad_src_keys: bfloat16 [4096, 4096], P('seq', 'heads')
- grad_src_values: bfloat16 [4096, 4096], P('seq', 'heads')
- grad_gain: float32 [4096], P('heads')
All inputs are finite; a program needn't handle non-finite values.
Results may differ from a plain program's by a relative error of at most 0.00115.
Values may be sent and summed in bfloat16 or wider, within the bound.
No kernel may reach another device: no remote copies, remote signals or barrier semaphores. Data moves between devices by JAX's collectives and lax.ppermute only.
A program may use at most 64 MiB of HBM per device.

v0:
```python
import math

import jax
import jax.numpy as jnp
from jax import lax
from jax.sharding import PartitionSpec as P

DH = 128


highest = lax.Precision.HIGHEST


def entering(part, axis, combine, identity, reverse):
    count = lax.axis_size(axis)
    place = lax.axis_index(axis)
    ahead = count - 1 - place if reverse else place
    gathered = lax.all_gather(part, axis)
    state = jnp.zeros_like(part) + jnp.asarray(identity, part.dtype)

    def one(step, state):
        source = count - 1 - step if reverse else step
        return combine(state, lax.dynamic_index_in_dim(gathered, source, 0, False))

    return lax.fori_loop(0, ahead, one, state)


def narrow_outer(key_rows, value_rows):
    return jnp.einsum("shd,she->hde", key_rows, value_rows, preferred_element_type=jnp.float32)


def add_states(earlier, later):
    return earlier + later


def on_device(queries, keys, values, src_keys, src_values, norm_gain, out_weight, grad_out):
    length = queries.shape[0]
    src_length = src_keys.shape[0]
    head_count = queries.shape[1] // DH
    seq_count = lax.axis_size("seq")
    self_scale = 1.0 / math.sqrt(DH * length * seq_count)
    cross_scale = 1.0 / math.sqrt(DH * src_length * seq_count)
    query_narrow = queries.reshape(length, head_count, DH)
    key_narrow = keys.reshape(length, head_count, DH)
    value_narrow = values.reshape(length, head_count, DH)
    src_key_narrow = src_keys.reshape(src_length, head_count, DH)
    src_value_narrow = src_values.reshape(src_length, head_count, DH)
    query_rows = query_narrow.astype(jnp.float32)
    key_rows = key_narrow.astype(jnp.float32)
    value_rows = value_narrow.astype(jnp.float32)
    src_key_rows = src_key_narrow.astype(jnp.float32)
    src_value_rows = src_value_narrow.astype(jnp.float32)
    gain_rows = norm_gain.reshape(head_count, DH)
    own_state = narrow_outer(key_narrow, value_narrow)
    own_source = narrow_outer(src_key_narrow, src_value_narrow)
    empty = jnp.zeros((head_count, DH, DH), jnp.float32)
    before = entering(own_state, "seq", add_states, empty, False)
    source_state = lax.psum(own_source, "seq")
    scores = jnp.einsum(
        "thd,shd->hts", query_narrow, key_narrow, preferred_element_type=jnp.float32
    )
    causal = (
        lax.broadcasted_iota(jnp.int32, (length, length), 0)
        >= lax.broadcasted_iota(jnp.int32, (length, length), 1)
    ).astype(jnp.float32)
    masked = scores * causal[None]
    within = jnp.einsum("hts,she->the", masked, value_rows, precision=highest)
    earlier = jnp.einsum("thd,hde->the", query_rows, before, precision=highest)
    crossed = jnp.einsum("thd,hde->the", query_rows, source_state, precision=highest)
    mixture = (within + earlier) * self_scale + crossed * cross_scale
    inverse = lax.rsqrt(jnp.mean(mixture * mixture, axis=-1, keepdims=True) + 1e-06)
    normed = mixture * inverse * gain_rows[None]
    grad_normed = lax.dot_general(
        lax.all_gather(grad_out, "heads", axis=1, tiled=True),
        out_weight,
        (((1,), (1,)), ((), ())),
        preferred_element_type=jnp.float32,
    )
    grad_normed = grad_normed.reshape(length, head_count, DH)
    grad_gain = jnp.sum(grad_normed * mixture * inverse, axis=0)
    gained = grad_normed * gain_rows[None]
    inner = jnp.mean(gained * mixture, axis=-1, keepdims=True)
    grad_mixture = inverse * gained - mixture * (inverse * inverse * inverse) * inner
    grad_self = grad_mixture * self_scale
    grad_cross = grad_mixture * cross_scale
    grad_scores = (
        jnp.einsum("the,she->hts", grad_self, value_rows, precision=highest) * causal[None]
    )
    grad_value = jnp.einsum("hts,the->she", masked, grad_self, precision=highest)
    grad_query = (
        jnp.einsum("hts,shd->thd", grad_scores, key_rows, precision=highest)
        + jnp.einsum("the,hde->thd", grad_self, before, precision=highest)
        + jnp.einsum("the,hde->thd", grad_cross, source_state, precision=highest)
    )
    grad_key = jnp.einsum("hts,thd->shd", grad_scores, query_rows, precision=highest)
    grad_before = jnp.einsum("thd,the->hde", query_rows, grad_self, precision=highest)
    grad_source = jnp.einsum("thd,the->hde", query_rows, grad_cross, precision=highest)
    later_state = entering(grad_before, "seq", add_states, empty, True)
    source_total, gain_total = lax.psum((grad_source, grad_gain), "seq")
    grad_key = grad_key + jnp.einsum("she,hde->shd", value_rows, later_state, precision=highest)
    grad_value = grad_value + jnp.einsum("shd,hde->she", key_rows, later_state, precision=highest)
    grad_src_key = jnp.einsum("she,hde->shd", src_value_rows, source_total, precision=highest)
    grad_src_value = jnp.einsum("shd,hde->she", src_key_rows, source_total, precision=highest)
    width = head_count * DH
    return (
        normed.reshape(length, width).astype(jnp.bfloat16),
        grad_query.reshape(length, width).astype(jnp.bfloat16),
        grad_key.reshape(length, width).astype(jnp.bfloat16),
        grad_value.reshape(length, width).astype(jnp.bfloat16),
        grad_src_key.reshape(src_length, width).astype(jnp.bfloat16),
        grad_src_value.reshape(src_length, width).astype(jnp.bfloat16),
        gain_total.reshape(width),
    )


def solution(mesh):
    placed = (
        P("seq", "heads"),
        P("seq", "heads"),
        P("seq", "heads"),
        P("seq", "heads"),
        P("seq", "heads"),
        P("heads"),
        P("heads", None),
        P("seq", "heads"),
    )
    return jax.shard_map(
        on_device,
        mesh=mesh,
        in_specs=placed,
        out_specs=(
            P("seq", "heads"),
            P("seq", "heads"),
            P("seq", "heads"),
            P("seq", "heads"),
            P("seq", "heads"),
            P("seq", "heads"),
            P("heads"),
        ),
        check_vma=False,
    )
```

profile of v0, /device:TPU:16, one launch (start us, length us, event | category | flops | bytes accessed | tf_op | source)
XLA Modules:
  0.0 587.0 jit_solution(10531398994005573377)
XLA Ops:
  8.0 1.0 copy.155
  9.0 1.8 fusion.21
  10.8 1.7 fusion.44
  12.7 1.3 convolution_multiply_fusion
  14.0 43.4 %all-gather.6.cloned.1.call-done = bf16[256,4096]{1,0:T(8,128)(2,1)} async-done(((bf16[256,256]{1,0:T(8,128)(2,1)}), bf16[256,4096]{1,0:T(8,128)(2,1)}) %all-gather.6.cloned.1.call-update) | async-done | bytes 2097168 | tf_op jit(solution)/shard_map/all_gather | solution.py:74
  57.4 2.3 fusion.64
  59.8 89.9 %all-gather.8.cloned.1.call-done = f32[64,128,128]{2,1,0:T(8,128)} async-done(((f32[2,128,128]{2,1,0:T(8,128)}), f32[64,128,128]{2,1,0:T(8,128)}) %all-gather.8.cloned.1.call-update) | async-done | bytes 4194320 | tf_op jit(solution)/shard_map/all_gather | solution.py:18
  150.5 151.6 %all-reduce.3.cloned.1.call-done = f32[2,128,128]{2,1,0:T(8,128)} async-done(((f32[2,128,128]{2,1,0:T(8,128)}), f32[2,128,128]{2,1,0:T(8,128)}) %all-reduce.3.cloned.1.call-update) | async-done | bytes 131088 | tf_op jit(solution)/shard_map/psum | solution.py:58
  302.2 1.2 multiply_reduce_fusion.2
  306.5 1.4 convolution_multiply_fusion.1
  308.0 1.3 convolution_bitcast_fusion.3
  309.7 1.3 fusion.7
  311.8 73.6 %psum.23 = f32[256]{0:T(256)} all-reduce(f32[256]{0:T(256)S(1)} %bitcast.183), channel_id=1, replica_groups=mesh['heads'=16,'seq'=32] {'seq'}, use_global_device_ids=true, to_apply=%region_9.10 | all-reduce | flops 256 | bytes 2048 | tf_op jit(solution)/shard_map/psum | solution.py:99
  385.3 1.2 fusion.13
  386.5 70.0 %all-reduce.5.cloned.1.call-done = f32[2,128,128]{1,2,0:T(8,128)} async-done(((f32[2,128,128]{1,2,0:T(8,128)}), f32[2,128,128]{1,2,0:T(8,128)}) %all-reduce.5.cloned.1.call-update) | async-done | bytes 131088 | tf_op jit(solution)/shard_map/psum | solution.py:99
  456.5 1.2 convolution_convert_fusion.1
  458.4 1.2 convolution_convert_fusion
  460.4 86.2 %all-gather.10.cloned.1.call-done = f32[64,128,128]{2,1,0:T(8,128)} async-done(((f32[2,128,128]{2,1,0:T(8,128)}), f32[64,128,128]{2,1,0:T(8,128)}) %all-gather.10.cloned.1.call-update) | async-done | bytes 4194320 | tf_op jit(solution)/shard_map/all_gather | solution.py:18
  546.6 29.8 %while.23 = (s32[]{:T(128)}, f32[2,128,128]{2,1,0:T(8,128)S(1)}, s32[]{:T(128)}, f32[32,2,128,128]{3,2,1,0:T(8,128)}, s32[]{:T(128)}, /*index=5*/s32[]{:T(128)}, s32[]{:T(128)}, s32[]{:T(128)}) while((s32[]{:T(128)}, f32[2,128,128]{2,1,0:T(8,128)S(1)}, s32[]{:T(128)}, f32[32,2,128,128]{3,2,1,0:T(8,128)}, s32[]{:T(128)}, /*index=5*/s32[]{:T(128)}, ...), condition=%wide.region_6.7_spmd, body=%wide.region_5.6_spmd.sunk | while | flops 32774 | bytes 393359 | solution.py:25
  546.6 0.9 bitcast_add_fusion.5
  549.5 0.9 bitcast_add_fusion.5
  564.8 0.9 bitcast_add_fusion.5
  576.3 1.0 convolution_bitcast_fusion.5
  578.4 1.3 fusion.8
  (79 shorter events, 35.5 us)
Async XLA Ops:
  7.2 50.2 %copy-start = (bf16[256,4096]{1,0:T(8,128)(2,1)S(1)}, bf16[256,4096]{1,0:T(8,128)(2,1)}, u32[]{:S(2)}) copy-start(bf16[256,4096]{1,0:T(8,128)(2,1)} %param.18) | copy-start | bytes 6291460
  7.2 50.2 %all-gather.6.cloned.1.call-start = ((), (), s32[]{:S(2)}) async-start(), calls=%async_computation.1 | async-start | bytes 2228224 | tf_op jit(solution)/shard_map/all_gather | solution.py:74
  7.9 141.8 %all-gather.8.cloned.1.call-start = ((), (), s32[]{:S(2)}) async-start(), calls=%async_computation.3 | async-start | bytes 4325376 | tf_op jit(solution)/shard_map/all_gather | solution.py:18
  9.0 3.7 copy-start.6
  10.8 291.4 %all-reduce.3.cloned.1.call-start = ((), (), s32[]{:S(2)}) async-start(), calls=%async_computation | async-start | bytes 262144 | tf_op jit(solution)/shard_map/psum | solution.py:58
  12.6 443.9 %all-reduce.5.cloned.1.call-start = ((), (), s32[]{:S(2)}) async-start(), calls=%async_computation.2 | async-start | bytes 262144 | tf_op jit(solution)/shard_map/psum | solution.py:99
  12.7 44.7 %copy-start.3 = (f32[256,256]{1,0:T(8,128)}, f32[256,256]{1,0:T(8,128)S(1)}, u32[]{:S(2)}) copy-start(f32[256,256]{1,0:T(8,128)S(1)} %fusion.10) | copy-start | bytes 786436
  59.8 90.0 %copy-start.1 = (bf16[256,256]{1,0:T(8,128)(2,1)S(1)}, bf16[256,256]{1,0:T(8,128)(2,1)}, u32[]{:S(2)}) copy-start(bf16[256,256]{1,0:T(8,128)(2,1)} %param.12) | copy-start | bytes 393220
  59.8 90.3 %copy-start.4 = (bf16[256,256]{1,0:T(8,128)(2,1)S(1)}, bf16[256,256]{1,0:T(8,128)(2,1)}, u32[]{:S(2)}) copy-start(bf16[256,256]{1,0:T(8,128)(2,1)} %param.14) | copy-start | bytes 393220
  149.7 153.7 %copy-start.9 = (f32[256]{0:T(256)S(1)}, f32[256]{0:T(256)}, u32[]{:S(2)}) copy-start(f32[256]{0:T(256)} %param.17) | copy-start | bytes 3076
  304.7 241.9 %all-gather.10.cloned.1.call-start = ((), (), s32[]{:S(2)}) async-start(), calls=%async_computation.4 | async-start | bytes 4325376 | tf_op jit(solution)/shard_map/all_gather | solution.py:18
  311.7 264.6 %copy-start.5 = (bf16[256,256]{1,0:T(8,128)(2,1)S(1)}, bf16[256,256]{1,0:T(8,128)(2,1)}, u32[]{:S(2)}) copy-start(bf16[256,256]{1,0:T(8,128)(2,1)} %param.14) | copy-start | bytes 393220
  386.5 190.8 %copy-start.7 = (bf16[256,256]{1,0:T(8,128)(2,1)S(1)}, bf16[256,256]{1,0:T(8,128)(2,1)}, u32[]{:S(2)}) copy-start(bf16[256,256]{1,0:T(8,128)(2,1)} %param.13) | copy-start | bytes 393220
  386.5 190.8 %copy-start.8 = (f32[2,128,256]{2,1,0:T(8,128)S(1)}, f32[2,128,256]{2,1,0:T(8,128)}, u32[]{:S(2)}) copy-start(f32[2,128,256]{2,1,0:T(8,128)} %fusion.13) | copy-start | bytes 786436
  458.4 120.0 %copy-start.2 = (bf16[256,256]{1,0:T(8,128)(2,1)S(1)}, bf16[256,256]{1,0:T(8,128)(2,1)}, u32[]{:S(2)}) copy-start(bf16[256,256]{1,0:T(8,128)(2,1)} %param.12) | copy-start | bytes 393220
Sparse Core Ops, SparseCore 0:
  10.1 47.3 all-gather.5
  61.1 88.5 all-gather.7
  153.7 148.3 all-reduce.2
  306.4 150.0 all-reduce.4
  460.1 86.4 all-gather.9
where the time goes:
time: 588 us; the launch traced here: 587 us
  waiting for transfers between devices  442 us (75%)
  blocking collectives  73.6 us (13%)
  other arithmetic  29.4 us (5%)
  matrix products  20.9 us (4%)
  between operations  14 us (2%)
  local copies, waits for them, and re-layouts  6.36 us (1%)
    all_gather x2, waiting for transfers between devices, entering(): gathered = lax.all_gather(part, axis)  176 us
    psum x1, waiting for transfers between devices, on_device(): source_state = lax.psum(own_source, 'seq')  152 us
    psum x1, blocking collectives, on_device(): source_total, gain_total = lax.psum((grad_source, grad_gain), 'seq')  73.6 us
    psum x1, waiting for transfers between devices, on_device(): source_total, gain_total = lax.psum((grad_source, grad_gain), 'seq')  70 us
    all_gather x1, waiting for transfers between devices, on_device(): lax.all_gather(grad_out, 'heads', axis=1, tiled=True)  43.4 us
    add x31, other arithmetic, add_states(): return earlier + later  29 us
  transfers between devices with their start and end apart: 5, of which 5 were waited for; matrix products, arithmetic and copies ran while one was open for 4% of the time, Pallas kernels for 0%

commit v1 on v0

v1 whole, which is shorter than its diff:
```python
import functools
import math

import jax
import jax.numpy as jnp
from jax import lax
from jax.experimental import pallas as pl
from jax.experimental.pallas import tpu as pltpu
from jax.sharding import PartitionSpec as P

DH = 128
f32 = jnp.float32
bf16 = jnp.bfloat16
MIB = 1024 * 1024


def dot(a, b, over_a, over_b):
    return lax.dot_general(a, b, (((over_a,), (over_b,)), ((), ())), preferred_element_type=f32)


def halves(x):
    high = x.astype(bf16)
    return high, (x - high.astype(f32)).astype(bf16)


def head(h):
    return slice(h * DH, (h + 1) * DH)


def states_kernel(k_ref, v_ref, sk_ref, sv_ref, out_ref, *, heads, rows):
    per = DH // rows
    for h in range(heads):
        own = dot(k_ref[:, head(h)], v_ref[:, head(h)], 0, 0)
        source = dot(sk_ref[:, head(h)], sv_ref[:, head(h)], 0, 0)
        out_ref[h * per : (h + 1) * per, :rows, :] = own.reshape(per, rows, DH)
        out_ref[h * per : (h + 1) * per, rows:, :] = source.reshape(per, rows, DH)


def prefix_kernel(in_ref, out_ref, *, count, rows, self_scale, cross_scale):
    total = in_ref[0, rows:, :]
    for j in range(1, count):
        total = total + in_ref[j, rows:, :]
    state = total * cross_scale
    for j in range(count):
        out_ref[j] = state
        state = state + in_ref[j, :rows, :] * self_scale


def forward_kernel(q_ref, k_ref, v_ref, c_ref, gain_ref, att_ref, mix_ref, high_ref, low_ref, *, heads, self_scale):
    length = q_ref.shape[0]
    causal = lax.broadcasted_iota(jnp.int32, (length, length), 0) >= lax.broadcasted_iota(jnp.int32, (length, length), 1)
    for h in range(heads):
        q, k, v = q_ref[:, head(h)], k_ref[:, head(h)], v_ref[:, head(h)]
        masked = jnp.where(causal, dot(q, k, 1, 1), 0.0) * self_scale
        high, low = halves(masked)
        high_ref[h] = high
        low_ref[h] = low
        c_high, c_low = halves(c_ref[head(h), :])
        mixture = dot(high, v, 1, 0) + dot(low, v, 1, 0) + dot(q, c_high, 1, 0) + dot(q, c_low, 1, 0)
        mix_ref[:, head(h)] = mixture
        inverse = lax.rsqrt(jnp.mean(mixture * mixture, axis=-1, keepdims=True) + 1e-06)
        att_ref[:, head(h)] = (mixture * inverse * gain_ref[h : h + 1, :]).astype(bf16)


def cotangent_kernel(g_ref, w_ref, q_ref, mix_ref, gain_ref, out_ref, high_ref, low_ref, *, heads, rows, groups):
    width = g_ref.shape[2]
    grad_normed = dot(g_ref[0], w_ref[:, :width], 1, 1)
    for b in range(1, groups):
        grad_normed = grad_normed + dot(g_ref[b], w_ref[:, b * width : (b + 1) * width], 1, 1)
    per = DH // rows
    gains = []
    for h in range(heads):
        mixture = mix_ref[:, head(h)]
        inverse = lax.rsqrt(jnp.mean(mixture * mixture, axis=-1, keepdims=True) + 1e-06)
        part = grad_normed[:, head(h)]
        gains.append(jnp.sum(part * (mixture * inverse), axis=0, keepdims=True))
        gained = part * gain_ref[h : h + 1, :]
        inner = jnp.mean(gained * mixture, axis=-1, keepdims=True)
        grad_mixture = inverse * gained - mixture * (inverse * inverse * inverse * inner)
        high, low = halves(grad_mixture)
        high_ref[:, head(h)] = high
        low_ref[:, head(h)] = low
        q = q_ref[:, head(h)]
        outer = dot(q, high, 0, 0) + dot(q, low, 0, 0)
        out_ref[h * per : (h + 1) * per, :rows, :] = outer.reshape(per, rows, DH)
    gain = jnp.concatenate(gains + [jnp.zeros((rows - heads, DH), f32)], axis=0)
    out_ref[:, rows:, :] = jnp.broadcast_to(gain[None], (heads * per, rows, DH))


def local_kernel(q_ref, k_ref, v_ref, c_ref, mh_ref, ml_ref, gh_ref, gl_ref, gq_ref, gk_ref, gv_ref, *, heads, self_scale):
    length = q_ref.shape[0]
    causal = lax.broadcasted_iota(jnp.int32, (length, length), 0) >= lax.broadcasted_iota(jnp.int32, (length, length), 1)
    for h in range(heads):
        q, k, v = q_ref[:, head(h)], k_ref[:, head(h)], v_ref[:, head(h)]
        high, low = gh_ref[:, head(h)], gl_ref[:, head(h)]
        scores = jnp.where(causal, dot(high, v, 1, 1) + dot(low, v, 1, 1), 0.0) * self_scale
        s_high, s_low = halves(scores)
        c_high, c_low = halves(c_ref[head(h), :])
        m_high, m_low = mh_ref[h], ml_ref[h]
        grad_query = dot(s_high, k, 1, 0) + dot(s_low, k, 1, 0)
        grad_query = grad_query + dot(high, c_high, 1, 1) + dot(high, c_low, 1, 1) + dot(low, c_high, 1, 1)
        gq_ref[:, head(h)] = grad_query.astype(bf16)
        gk_ref[:, head(h)] = dot(s_high, q, 0, 0) + dot(s_low, q, 0, 0)
        gv_ref[:, head(h)] = dot(m_high, high, 0, 0) + dot(m_high, low, 0, 0) + dot(m_low, high, 0, 0)


def suffix_kernel(in_ref, out_ref, gain_ref, *, count, rows, heads, self_scale, cross_scale):
    gain = in_ref[0, rows:, :]
    for j in range(1, count):
        gain = gain + in_ref[j, rows:, :]
    gain_ref[...] = gain[:heads, :]
    state = jnp.zeros((rows, DH), f32)
    for j in range(count - 1, -1, -1):
        out_ref[j, :rows, :] = state * self_scale
        state = state + in_ref[j, :rows, :]
    total = state * cross_scale
    for j in range(count):
        out_ref[j, rows:, :] = total


def final_kernel(k_ref, v_ref, sk_ref, sv_ref, s_ref, gk_ref, gv_ref, out_k, out_v, out_sk, out_sv, *, heads, rows):
    per = DH // rows
    for h in range(heads):
        later = s_ref[h * per : (h + 1) * per, :rows, :].reshape(DH, DH)
        total = s_ref[h * per : (h + 1) * per, rows:, :].reshape(DH, DH)
        l_high, l_low = halves(later)
        t_high, t_low = halves(total)
        k, v, sk, sv = k_ref[:, head(h)], v_ref[:, head(h)], sk_ref[:, head(h)], sv_ref[:, head(h)]
        out_k[:, head(h)] = (gk_ref[:, head(h)] + dot(v, l_high, 1, 1) + dot(v, l_low, 1, 1)).astype(bf16)
        out_v[:, head(h)] = (gv_ref[:, head(h)] + dot(k, l_high, 1, 0) + dot(k, l_low, 1, 0)).astype(bf16)
        out_sk[:, head(h)] = (dot(sv, t_high, 1, 1) + dot(sv, t_low, 1, 1)).astype(bf16)
        out_sv[:, head(h)] = (dot(sk, t_high, 1, 0) + dot(sk, t_low, 1, 0)).astype(bf16)


def call(kernel, outs, name, **static):
    whole = pl.BlockSpec(memory_space=pltpu.VMEM)
    shapes = [jax.ShapeDtypeStruct(shape, dtype) for shape, dtype in outs]

    def run(*operands):
        return pl.pallas_call(
            functools.partial(kernel, **static),
            out_shape=shapes,
            in_specs=[whole] * len(operands),
            out_specs=[whole] * len(shapes),
            compiler_params=pltpu.CompilerParams(vmem_limit_bytes=24 * MIB),
            name=name,
        )(*operands)

    return run


def on_device(queries, keys, values, src_keys, src_values, norm_gain, out_weight, grad_out):
    length, width = queries.shape
    src_length = src_keys.shape[0]
    heads = width // DH
    count = lax.axis_size("seq")
    groups = lax.axis_size("heads")
    rows = width // count
    self_scale = 1.0 / math.sqrt(DH * length * count)
    cross_scale = 1.0 / math.sqrt(DH * src_length * count)
    gain = norm_gain.reshape(heads, DH)

    gathered = lax.all_gather(grad_out, "heads")
    (own,) = call(states_kernel, [((count, 2 * rows, DH), f32)], "states", heads=heads, rows=rows)(keys, values, src_keys, src_values)
    own = lax.all_to_all(own, "seq", 0, 0)
    (before,) = call(
        prefix_kernel, [((count, rows, DH), f32)], "prefix", count=count, rows=rows, self_scale=self_scale, cross_scale=cross_scale
    )(own)
    before = lax.all_to_all(before, "seq", 0, 0).reshape(width, DH)
    attended, mixture, m_high, m_low = call(
        forward_kernel,
        [((length, width), bf16), ((length, width), f32), ((heads, length, length), bf16), ((heads, length, length), bf16)],
        "forward",
        heads=heads,
        self_scale=self_scale,
    )(queries, keys, values, before, gain)
    outer, g_high, g_low = call(
        cotangent_kernel,
        [((count, 2 * rows, DH), f32), ((length, width), bf16), ((length, width), bf16)],
        "cotangent",
        heads=heads,
        rows=rows,
        groups=groups,
    )(gathered, out_weight, queries, mixture, gain)
    outer = lax.all_to_all(outer, "seq", 0, 0)
    grad_query, grad_key, grad_value = call(
        local_kernel,
        [((length, width), bf16), ((length, width), f32), ((length, width), f32)],
        "local",
        heads=heads,
        self_scale=self_scale,
    )(queries, keys, values, before, m_high, m_low, g_high, g_low)
    later, grad_gain = call(
        suffix_kernel,
        [((count, 2 * rows, DH), f32), ((heads, DH), f32)],
        "suffix",
        count=count,
        rows=rows,
        heads=heads,
        self_scale=self_scale,
        cross_scale=cross_scale,
    )(outer)
    later = lax.all_to_all(later, "seq", 0, 0)
    grad_key, grad_value, grad_src_key, grad_src_value = call(
        final_kernel,
        [((length, width), bf16), ((length, width), bf16), ((src_length, width), bf16), ((src_length, width), bf16)],
        "final",
        heads=heads,
        rows=rows,
    )(keys, values, src_keys, src_values, later, grad_key, grad_value)
    return attended, grad_query, grad_key, grad_value, grad_src_key, grad_src_value, grad_gain.reshape(width)


def solution(mesh):
    block = P("seq", "heads")
    return jax.shard_map(
        on_device,
        mesh=mesh,
        in_specs=(block, block, block, block, block, P("heads"), P("heads", None), block),
        out_specs=(block, block, block, block, block, block, P("heads")),
        check_vma=False,
    )
```

time: 588 us -> 110 us (0.19)
  the two profiles are of different devices: /device:TPU:16 before, /device:TPU:8 now
where the time goes in v1:
time: 110 us
  blocking collectives  63.2 us (57%)
  between operations  14.1 us (13%)
  local copies, waits for them, and re-layouts  11.6 us (11%)
  waiting for transfers between devices  10.4 us (9%)
  Pallas kernels  6.39 us (6%)
  starting transfers between devices  3.9 us (4%)
    all_to_all x1, blocking collectives, on_device(): own = lax.all_to_all(own, 'seq', 0, 0)  25.6 us
    all_to_all x1, blocking collectives, on_device(): outer = lax.all_to_all(outer, 'seq', 0, 0)  23.1 us
    all_to_all x1, blocking collectives, on_device(): before = lax.all_to_all(before, 'seq', 0, 0).reshape(width, DH)  14.5 us
    unnamed x38, local copies, waits for them, and re-layouts  11.6 us
    all_to_all x1, waiting for transfers between devices, on_device(): later = lax.all_to_all(later, 'seq', 0, 0)  9.69 us
    pallas_call x7, Pallas kernels, run(): pl.pallas_call(functools.partial(kernel, **static), out_shape=shapes, in_...  6.39 us
    all_to_all x1, starting transfers between devices, on_device(): later = lax.all_to_all(later, 'seq', 0, 0)  3.87 us
  transfers between devices with their start and end apart: 2, of which 1 were waited for; matrix products, arithmetic and copies ran while one was open for 0% of the time, Pallas kernels for 3%

profile of v1, /device:TPU:8, one launch (start us, length us, event | category | flops | bytes accessed | tf_op | source)
XLA Modules:
  0.0 109.7 jit_solution(14364060880499729535)
XLA Ops:
  7.2 0.7 all-gather.3.cloned.1.call-update
  7.9 0.9 copy-done.2
  8.8 0.9 copy-done.5
  9.7 0.8 copy-done.11
  10.6 0.8 copy-done.13
  11.7 25.6 %all_to_all.20.in_ref = f32[32,16,128]{2,1,0:T(8,128)S(1)} all-to-all(f32[32,16,128]{2,1,0:T(8,128)S(1)} %states.1), channel_id=1, replica_groups=mesh['heads'=16,'seq'=32] {'seq'}, dimensions={0} | all-to-all | bytes 524288 | tf_op jit(solution)/shard_map/all_to_all | solution.py:165
  37.4 14.5 %all_to_all.21 = f32[32,8,128]{2,1,0:T(8,128)S(1)} all-to-all(f32[32,8,128]{2,1,0:T(8,128)S(1)} %prefix.1), channel_id=1, replica_groups=mesh['heads'=16,'seq'=32] {'seq'}, dimensions={0} | all-to-all | bytes 262144 | tf_op jit(solution)/shard_map/all_to_all | solution.py:169
  51.9 0.9 copy-done.3
  52.8 0.9 copy-done.6
  53.7 0.9 copy-done.8
  54.6 0.7 copy-done.17
  55.3 1.4 %forward.1 = (bf16[256,256]{1,0:T(8,128)(2,1)}, f32[256,256]{1,0:T(8,128)S(1)}, bf16[2,256,256]{2,1,0:T(8,128)(2,1)S(1)}, bf16[2,256,256]{2,1,0:T(8,128)(2,1)S(1)}) custom-call(bf16[256,256]{1,0:T(8,128)(2,1)S(1)} %copy-done.8, bf16[256,256]{1,0:T(8,128)(2,1)S(1)} %copy-done.3, bf16[256,256]{1,0:T(8,128)(2,1)S(1)} %copy-done.6, f32[256,128]{1,0:T(8,128)S(1)} %bitcast.5, ...), custom_call_target="tpu_custom_call" | custom-call | tf_op jit(solution)/shard_map/forward/pallas_call | solution.py:140
  56.7 1.6 %copy-done.1 = bf16[4096,256]{1,0:T(8,128)(2,1)S(1)} copy-done((bf16[4096,256]{1,0:T(8,128)(2,1)S(1)}, bf16[4096,256]{1,0:T(8,128)(2,1)}, u32[]{:S(2)}) %copy-start.1) | copy-done | bytes 2097176
  58.3 0.9 copy-done.9
  59.2 0.7 copy-done.18
  59.9 1.2 %cotangent.1 = (f32[32,16,128]{2,1,0:T(8,128)S(1)}, bf16[256,256]{1,0:T(8,128)(2,1)S(1)}, bf16[256,256]{1,0:T(8,128)(2,1)S(1)}) custom-call(bf16[16,256,256]{2,1,0:T(8,128)(2,1)S(1)} %bitcast.4, bf16[256,4096]{1,0:T(8,128)(2,1)S(1)} %copy-done, bf16[256,256]{1,0:T(8,128)(2,1)S(1)} %copy-done.9, f32[256,256]{1,0:T(8,128)S(1)} %get-tuple-element.26.mix_ref, ...), custom_call_target="tpu_custom_call" | custom-call | tf_op jit(solution)/shard_map/cotangent/pallas_call | solution.py:140
  61.1 0.6 copy-done.15
  61.7 23.1 %all_to_all.22.in_ref = f32[32,16,128]{2,1,0:T(8,128)S(1)} all-to-all(f32[32,16,128]{2,1,0:T(8,128)S(1)} %get-tuple-element.30), channel_id=1, replica_groups=mesh['heads'=16,'seq'=32] {'seq'}, dimensions={0} | all-to-all | bytes 524288 | tf_op jit(solution)/shard_map/all_to_all | solution.py:185
  84.8 0.8 suffix.1
  85.6 3.9 %all-to-all-start.3 = ((f32[32,16,128]{2,1,0:T(8,128)}), f32[32,16,128]{2,1,0:T(8,128)S(1)}, u32[]{:S(2)}, u32[]{:S(2)}) async-start(f32[32,16,128]{2,1,0:T(8,128)} %get-tuple-element.31), calls=%async_computation.3 | async-start | bytes 524288 | tf_op jit(solution)/shard_map/all_to_all | solution.py:203
  89.5 0.9 copy-done.16
  90.4 1.6 %local.1 = (bf16[256,256]{1,0:T(8,128)(2,1)}, f32[256,256]{1,0:T(8,128)S(1)}, f32[256,256]{1,0:T(8,128)S(1)}) custom-call(bf16[256,256]{1,0:T(8,128)(2,1)S(1)} %copy-done.10, bf16[256,256]{1,0:T(8,128)(2,1)S(1)} %copy-done.4, bf16[256,256]{1,0:T(8,128)(2,1)S(1)} %copy-done.7, f32[256,128]{1,0:T(8,128)S(1)} %bitcast.6, ...), custom_call_target="tpu_custom_call" | custom-call | tf_op jit(solution)/shard_map/local/pallas_call | solution.py:140
  92.0 9.7 %all-to-all-done.3.s_ref = f32[32,16,128]{2,1,0:T(8,128)S(1)} async-done(((f32[32,16,128]{2,1,0:T(8,128)}), f32[32,16,128]{2,1,0:T(8,128)S(1)}, u32[]{:S(2)}, u32[]{:S(2)}) %all-to-all-start.3) | async-done | bytes 262176 | tf_op jit(solution)/shard_map/all_to_all | solution.py:203
  101.7 1.1 final.1
  (29 shorter events, 0.4 us)
Async XLA Ops:
  7.2 49.6 %copy-start = (bf16[256,4096]{1,0:T(8,128)(2,1)S(1)}, bf16[256,4096]{1,0:T(8,128)(2,1)}, u32[]{:S(2)}) copy-start(bf16[256,4096]{1,0:T(8,128)(2,1)} %w_ref.1) | copy-start | bytes 6291460
  7.2 49.6 %all-gather.3.cloned.1.call-start = ((), (), s32[]{:S(2)}) async-start(), calls=%async_computation.4 | async-start | bytes 2228224 | tf_op jit(solution)/shard_map/all_gather | solution.py:163
  7.9 0.9 copy-start.2
  8.8 0.9 copy-start.5
  9.7 0.8 copy-start.11
  10.6 0.8 copy-start.13
  51.9 0.9 copy-start.3
  52.8 0.9 copy-start.6
  53.7 0.9 copy-start.8
  54.6 0.7 copy-start.17
  56.7 1.6 %copy-start.1 = (bf16[4096,256]{1,0:T(8,128)(2,1)S(1)}, bf16[4096,256]{1,0:T(8,128)(2,1)}, u32[]{:S(2)}) copy-start(bf16[4096,256]{1,0:T(8,128)(2,1)} %all-gather.3.cloned.1.call-done) | copy-start | bytes 6291460
  58.3 0.9 copy-start.9
  59.2 0.7 copy-start.18
  59.9 29.5 %copy-start.4 = (bf16[256,256]{1,0:T(8,128)(2,1)S(1)}, bf16[256,256]{1,0:T(8,128)(2,1)}, u32[]{:S(2)}) copy-start(bf16[256,256]{1,0:T(8,128)(2,1)} %k_ref.7) | copy-start | bytes 393220
  59.9 29.5 %copy-start.7 = (bf16[256,256]{1,0:T(8,128)(2,1)S(1)}, bf16[256,256]{1,0:T(8,128)(2,1)}, u32[]{:S(2)}) copy-start(bf16[256,256]{1,0:T(8,128)(2,1)} %v_ref.7) | copy-start | bytes 393220
  59.9 29.5 %copy-start.10 = (bf16[256,256]{1,0:T(8,128)(2,1)S(1)}, bf16[256,256]{1,0:T(8,128)(2,1)}, u32[]{:S(2)}) copy-start(bf16[256,256]{1,0:T(8,128)(2,1)} %q_ref.5) | copy-start | bytes 393220
  61.1 0.7 copy-start.15
  61.7 40.0 %copy-start.12 = (bf16[128,256]{1,0:T(8,128)(2,1)S(1)}, bf16[128,256]{1,0:T(8,128)(2,1)}, u32[]{:S(2)}) copy-start(bf16[128,256]{1,0:T(8,128)(2,1)} %sk_ref.3) | copy-start | bytes 196612
  61.7 40.0 %copy-start.14 = (bf16[128,256]{1,0:T(8,128)(2,1)S(1)}, bf16[128,256]{1,0:T(8,128)(2,1)}, u32[]{:S(2)}) copy-start(bf16[128,256]{1,0:T(8,128)(2,1)} %sv_ref.3) | copy-start | bytes 196612
  85.6 16.2 %all-to-all-start.3 = ((f32[32,16,128]{2,1,0:T(8,128)}), f32[32,16,128]{2,1,0:T(8,128)S(1)}, u32[]{:S(2)}, u32[]{:S(2)}) async-start(f32[32,16,128]{2,1,0:T(8,128)} %get-tuple-element.31), calls=%async_computation.3 | async-start | bytes 524288 | tf_op jit(solution)/shard_map/all_to_all | solution.py:203
  89.5 0.9 copy-start.16
Sparse Core Ops, SparseCore 0:
  10.1 46.3 all-gather.2

commit v2 on v1

--- a/solution.py
+++ b/solution.py
@@ -27,13 +27,34 @@
     return slice(h * DH, (h + 1) * DH)
 
 
-def states_kernel(k_ref, v_ref, sk_ref, sv_ref, out_ref, *, heads, rows):
+def states_kernel(k_hbm, v_hbm, sk_hbm, sv_hbm, out_ref, k_ref, v_ref, sk_ref, sv_ref, sems, *, heads, rows):
+    pairs = ((k_hbm, k_ref), (v_hbm, v_ref), (sk_hbm, sk_ref), (sv_hbm, sv_ref))
+    loads = [pltpu.make_async_copy(a, b, sems.at[i]) for i, (a, b) in enumerate(pairs)]
+    for load in loads:
+        load.start()
     per = DH // rows
-    for h in range(heads):
-        own = dot(k_ref[:, head(h)], v_ref[:, head(h)], 0, 0)
-        source = dot(sk_ref[:, head(h)], sv_ref[:, head(h)], 0, 0)
-        out_ref[h * per : (h + 1) * per, :rows, :] = own.reshape(per, rows, DH)
-        out_ref[h * per : (h + 1) * per, rows:, :] = source.reshape(per, rows, DH)
+    for at, left, right in ((0, k_ref, v_ref), (1, sk_ref, sv_ref)):
+        loads[2 * at].wait()
+        loads[2 * at + 1].wait()
+        for h in range(heads):
+            state = dot(left[:, head(h)], right[:, head(h)], 0, 0)
+            out_ref[h * per : (h + 1) * per, at * rows : (at + 1) * rows, :] = state.reshape(per, rows, DH)
+
+
+def pack_kernel(*refs):
+    *parts, _, out_ref, sems = refs
+    copies, at = [], 0
+    for i, part in enumerate(parts):
+        copies.append(pltpu.make_async_copy(part, out_ref.at[at : at + part.shape[0]], sems.at[i]))
+        at += part.shape[0]
+    for copy in copies:
+        copy.start()
+    for copy in copies:
+        copy.wait()
+
+
+def gate_kernel(x_ref, *refs):
+    del x_ref, refs
 
 
 def prefix_kernel(in_ref, out_ref, *, count, rows, self_scale, cross_scale):
@@ -46,27 +67,48 @@
         state = state + in_ref[j, :rows, :] * self_scale
 
 
-def forward_kernel(q_ref, k_ref, v_ref, c_ref, gain_ref, att_ref, mix_ref, high_ref, low_ref, *, heads, self_scale):
-    length = q_ref.shape[0]
+def masked_scores(q, k, self_scale):
+    length = q.shape[0]
     causal = lax.broadcasted_iota(jnp.int32, (length, length), 0) >= lax.broadcasted_iota(jnp.int32, (length, length), 1)
-    for h in range(heads):
-        q, k, v = q_ref[:, head(h)], k_ref[:, head(h)], v_ref[:, head(h)]
-        masked = jnp.where(causal, dot(q, k, 1, 1), 0.0) * self_scale
-        high, low = halves(masked)
-        high_ref[h] = high
-        low_ref[h] = low
+    return causal, halves(jnp.where(causal, dot(q, k, 1, 1), 0.0) * self_scale)
+
+
+def within_kernel(q_ref, k_ref, v_ref, out_ref, *, heads, self_scale):
+    for h in range(heads):
+        v = v_ref[:, head(h)]
+        _, (high, low) = masked_scores(q_ref[:, head(h)], k_ref[:, head(h)], self_scale)
+        out_ref[:, head(h)] = dot(high, v, 1, 0) + dot(low, v, 1, 0)
+
+
+def forward_kernel(q_ref, within_ref, c_ref, gain_ref, att_ref, mix_ref, *, heads):
+    for h in range(heads):
+        q = q_ref[:, head(h)]
         c_high, c_low = halves(c_ref[head(h), :])
-        mixture = dot(high, v, 1, 0) + dot(low, v, 1, 0) + dot(q, c_high, 1, 0) + dot(q, c_low, 1, 0)
+        mixture = within_ref[:, head(h)] + dot(q, c_high, 1, 0) + dot(q, c_low, 1, 0)
         mix_ref[:, head(h)] = mixture
         inverse = lax.rsqrt(jnp.mean(mixture * mixture, axis=-1, keepdims=True) + 1e-06)
         att_ref[:, head(h)] = (mixture * inverse * gain_ref[h : h + 1, :]).astype(bf16)
 
 
-def cotangent_kernel(g_ref, w_ref, q_ref, mix_ref, gain_ref, out_ref, high_ref, low_ref, *, heads, rows, groups):
-    width = g_ref.shape[2]
-    grad_normed = dot(g_ref[0], w_ref[:, :width], 1, 1)
-    for b in range(1, groups):
-        grad_normed = grad_normed + dot(g_ref[b], w_ref[:, b * width : (b + 1) * width], 1, 1)
+def cotangent_kernel(place_ref, *refs, heads, rows, parts):
+    blocks = refs[: len(parts)]
+    w_ref, q_ref, mix_ref, gain_ref, out_ref, high_ref, low_ref = refs[len(parts) : len(parts) + 7]
+    held, sems = refs[len(parts) + 7 : -1], refs[-1]
+    loads = [pltpu.make_async_copy(a, b, sems.at[i]) for i, (a, b) in enumerate(zip(blocks, held))]
+    for load in loads:
+        load.start()
+    length, width = held[0].shape[1:]
+    chip, core = place_ref[0], place_ref[1]
+    chips = w_ref.shape[1] // (2 * width)
+    grad_normed = jnp.zeros((length, width), f32)
+    for load, ref, part in zip(loads, held, parts):
+        load.wait()
+        for b, (steps, swapped, which) in enumerate(part):
+            side = 1 - core if swapped else core
+            source = lax.rem(chip + chips + (2 * side - 1) * steps, chips)
+            at = 2 * source + (side if which is None else which)
+            columns = pl.ds(pl.multiple_of(at * width, width), width)
+            grad_normed = grad_normed + dot(ref[b], w_ref[:, columns], 1, 1)
     per = DH // rows
     gains = []
     for h in range(heads):
@@ -87,16 +129,14 @@
     out_ref[:, rows:, :] = jnp.broadcast_to(gain[None], (heads * per, rows, DH))
 
 
-def local_kernel(q_ref, k_ref, v_ref, c_ref, mh_ref, ml_ref, gh_ref, gl_ref, gq_ref, gk_ref, gv_ref, *, heads, self_scale):
-    length = q_ref.shape[0]
-    causal = lax.broadcasted_iota(jnp.int32, (length, length), 0) >= lax.broadcasted_iota(jnp.int32, (length, length), 1)
+def local_kernel(q_ref, k_ref, v_ref, c_ref, gh_ref, gl_ref, gq_ref, gk_ref, gv_ref, *, heads, self_scale):
     for h in range(heads):
         q, k, v = q_ref[:, head(h)], k_ref[:, head(h)], v_ref[:, head(h)]
         high, low = gh_ref[:, head(h)], gl_ref[:, head(h)]
+        causal, (m_high, m_low) = masked_scores(q, k, self_scale)
         scores = jnp.where(causal, dot(high, v, 1, 1) + dot(low, v, 1, 1), 0.0) * self_scale
         s_high, s_low = halves(scores)
         c_high, c_low = halves(c_ref[head(h), :])
-        m_high, m_low = mh_ref[h], ml_ref[h]
         grad_query = dot(s_high, k, 1, 0) + dot(s_low, k, 1, 0)
         grad_query = grad_query + dot(high, c_high, 1, 1) + dot(high, c_low, 1, 1) + dot(low, c_high, 1, 1)
         gq_ref[:, head(h)] = grad_query.astype(bf16)
@@ -132,21 +172,48 @@
         out_sv[:, head(h)] = (dot(sk, t_high, 1, 0) + dot(sk, t_low, 1, 0)).astype(bf16)
 
 
-def call(kernel, outs, name, **static):
-    whole = pl.BlockSpec(memory_space=pltpu.VMEM)
+WHOLE = pl.BlockSpec(memory_space=pltpu.VMEM)
+SCALAR = pl.BlockSpec(memory_space=pltpu.SMEM)
+ANY = pl.BlockSpec(memory_space=pl.ANY)
+HBM = pl.BlockSpec(memory_space=pltpu.HBM)
+
+
+MICROSECONDS = {"states": 10, "pack": 10, "within": 20, "forward": 2, "cotangent": 3, "local": 3}
+
+
+def call(kernel, outs, name, ins=None, scratch=(), aliases=None, out_specs=None, **static):
     shapes = [jax.ShapeDtypeStruct(shape, dtype) for shape, dtype in outs]
 
     def run(*operands):
         return pl.pallas_call(
             functools.partial(kernel, **static),
             out_shape=shapes,
-            in_specs=[whole] * len(operands),
-            out_specs=[whole] * len(shapes),
-            compiler_params=pltpu.CompilerParams(vmem_limit_bytes=24 * MIB),
+            in_specs=ins or [WHOLE] * len(operands),
+            out_specs=out_specs or [WHOLE] * len(shapes),
+            scratch_shapes=scratch,
+            input_output_aliases=aliases or {},
+            compiler_params=pltpu.CompilerParams(vmem_limit_bytes=12 * MIB),
             name=name,
+            cost_estimate=pl.CostEstimate(flops=0, transcendentals=0, bytes_accessed=int(MICROSECONDS.get(name, 0.5) * 3.69e6)),
         )(*operands)
 
     return run
+
+
+def pack(parts, after):
+    shape = (sum(part.shape[0] for part in parts), *parts[0].shape[1:])
+    return call(
+        pack_kernel,
+        [(shape, parts[0].dtype)],
+        "pack",
+        ins=[ANY] * (len(parts) + 1),
+        scratch=[pltpu.SemaphoreType.DMA((len(parts),))],
+    )(*parts, after)[0]
+
+
+def gate(x, *after):
+    outs = [(x.shape, x.dtype)]
+    return call(gate_kernel, outs, "gate", ins=[ANY] * (1 + len(after)), aliases={0: 0}, out_specs=[ANY])(x, *after)[0]
 
 
 def on_device(queries, keys, values, src_keys, src_values, norm_gain, out_weight, grad_out):
@@ -160,28 +227,54 @@
     cross_scale = 1.0 / math.sqrt(DH * src_length * count)
     gain = norm_gain.reshape(heads, DH)
 
-    gathered = lax.all_gather(grad_out, "heads")
-    (own,) = call(states_kernel, [((count, 2 * rows, DH), f32)], "states", heads=heads, rows=rows)(keys, values, src_keys, src_values)
+    chips = groups // 2
+    chip = lax.axis_index("heads") // 2
+    core = lax.axis_index("heads") % 2
+    place = jnp.stack([chip, core]).astype(jnp.int32)
+
+    def along(d):
+        return [(2 * y + c, 2 * ((y + (d if c == 0 else -d)) % chips) + c) for y in range(chips) for c in range(2)]
+
+    across = lax.ppermute(grad_out[None], "heads", along(chips // 2))
+    (own,) = call(
+        states_kernel,
+        [((count, 2 * rows, DH), f32)],
+        "states",
+        ins=[HBM] * 4,
+        scratch=[pltpu.VMEM(x.shape, x.dtype) for x in (keys, values, src_keys, src_values)] + [pltpu.SemaphoreType.DMA((4,))],
+        heads=heads,
+        rows=rows,
+    )(*(pltpu.with_memory_space_constraint(x, pltpu.HBM) for x in (keys, values, src_keys, src_values)))
+    held = jnp.concatenate([grad_out[None], across], axis=0)
+    held_next = lax.ppermute(held, "heads", along(2))
     own = lax.all_to_all(own, "seq", 0, 0)
     (before,) = call(
         prefix_kernel, [((count, rows, DH), f32)], "prefix", count=count, rows=rows, self_scale=self_scale, cross_scale=cross_scale
     )(own)
+    held = jnp.concatenate([held, gate(held_next, before)], axis=0)
+    got = lax.ppermute(held, "heads", along(1))
+    swap = [(i, i ^ 1) for i in range(groups)]
+    other_held = lax.ppermute(held, "heads", swap)
     before = lax.all_to_all(before, "seq", 0, 0).reshape(width, DH)
-    attended, mixture, m_high, m_low = call(
-        forward_kernel,
-        [((length, width), bf16), ((length, width), f32), ((heads, length, length), bf16), ((heads, length, length), bf16)],
-        "forward",
-        heads=heads,
-        self_scale=self_scale,
-    )(queries, keys, values, before, gain)
+    (within,) = call(within_kernel, [((length, width), f32)], "within", heads=heads, self_scale=self_scale)(queries, keys, values)
+    got = gate(got, before, within)
+    other_got = lax.ppermute(got, "heads", swap)
+    attended, mixture = call(forward_kernel, [((length, width), bf16), ((length, width), f32)], "forward", heads=heads)(
+        queries, within, before, gain
+    )
+    blocks = [held, other_held, got, other_got]
+    quad = [(0, None), (4, None), (2, None), (6, None)]
+    parts = [[((d + far) % chips, swapped, None) for d, _ in quad] for far in (0, 1) for swapped in (False, True)]
     outer, g_high, g_low = call(
         cotangent_kernel,
         [((count, 2 * rows, DH), f32), ((length, width), bf16), ((length, width), bf16)],
         "cotangent",
+        ins=[SCALAR] + [ANY] * len(blocks) + [WHOLE] * 4,
+        scratch=[pltpu.VMEM(x.shape, x.dtype) for x in blocks] + [pltpu.SemaphoreType.DMA((len(blocks),))],
         heads=heads,
         rows=rows,
-        groups=groups,
-    )(gathered, out_weight, queries, mixture, gain)
+        parts=parts,
+    )(place, *blocks, out_weight, queries, mixture, gain)
     outer = lax.all_to_all(outer, "seq", 0, 0)
     grad_query, grad_key, grad_value = call(
         local_kernel,
@@ -189,7 +282,7 @@
         "local",
         heads=heads,
         self_scale=self_scale,
-    )(queries, keys, values, before, m_high, m_low, g_high, g_low)
+    )(queries, keys, values, before, g_high, g_low)
     later, grad_gain = call(
         suffix_kernel,
         [((count, 2 * rows, DH), f32), ((heads, DH), f32)],

time: 110 us -> 103 us (0.936)
  the two profiles are of different devices: /device:TPU:8 before, /device:TPU:56 now
where the time goes in v2:
time: 103 us; the launch traced here: 102 us
  starting transfers between devices  45.9 us (45%)
  waiting for transfers between devices  26.5 us (26%)
  blocking collectives  16.6 us (16%)
  Pallas kernels  11.1 us (11%)
  other arithmetic  1.06 us (1%)
    all_to_all x1, blocking collectives, on_device(): outer = lax.all_to_all(outer, 'seq', 0, 0)  16.6 us
    all_to_all x1, starting transfers between devices, on_device(): own = lax.all_to_all(own, 'seq', 0, 0)  13.2 us
    pallas_call x10, Pallas kernels, run(): pl.pallas_call(functools.partial(kernel, **static), out_shape=shapes, in_...  11.1 us
    all_to_all x1, waiting for transfers between devices, on_device(): later = lax.all_to_all(later, 'seq', 0, 0)  10.6 us
    all_to_all x1, starting transfers between devices, on_device(): before = lax.all_to_all(before, 'seq', 0, 0).reshape(width, DH)  9.79 us
    all_to_all x1, waiting for transfers between devices, on_device(): before = lax.all_to_all(before, 'seq', 0, 0).reshape(width, DH)  8.05 us
    all_to_all x1, waiting for transfers between devices, on_device(): own = lax.all_to_all(own, 'seq', 0, 0)  6.81 us
    ppermute x1, starting transfers between devices, on_device(): got = lax.ppermute(held, 'heads', along(1))  5.57 us
  transfers between devices with their start and end apart: 8, of which 4 were waited for; matrix products, arithmetic and copies ran while one was open for 1% of the time, Pallas kernels for 6%

profile of v2, /device:TPU:56, one launch (start us, length us, event | category | flops | bytes accessed | tf_op | source)
XLA Modules:
  0.0 102.2 jit_solution(13139538436751792224)
XLA Ops:
  0.7 4.8 %collective-permute-start = (bf16[1,256,256]{2,1,0:T(8,128)(2,1)}, bf16[1,256,256]{2,1,0:T(8,128)(2,1)S(1)}, u32[]{:S(2)}, u32[]{:S(2)}) collective-permute-start(bf16[1,256,256]{2,1,0:T(8,128)(2,1)} %bitcast.11), channel_id=1, source_target_pairs={{0,256},{32,288},{64,320},{96,352},{128,384},{160,416},{192,448},{... | collective-permute-start | bytes 393224 | tf_op jit(solution)/shard_map/ppermute | solution.py:238
  5.5 2.1 %states.1 = f32[32,16,128]{2,1,0:T(8,128)} custom-call(bf16[256,256]{1,0:T(8,128)(2,1)} %k_ref.5, bf16[256,256]{1,0:T(8,128)(2,1)} %v_ref.5, bf16[128,256]{1,0:T(8,128)(2,1)} %sk_ref.1, bf16[128,256]{1,0:T(8,128)(2,1)} %sv_ref.1), custom_call_target="tpu_custom_call" | custom-call | bytes 36900000 | tf_op jit(solution)/shard_map/states/pallas_call | solution.py:188
  7.7 13.2 %all-to-all-start = ((f32[32,16,128]{2,1,0:T(8,128)}), f32[32,16,128]{2,1,0:T(8,128)S(1)}, u32[]{:S(2)}, u32[]{:S(2)}) async-start(f32[32,16,128]{2,1,0:T(8,128)} %states.1), calls=%async_computation | async-start | bytes 524288 | tf_op jit(solution)/shard_map/all_to_all | solution.py:250
  20.9 0.9 pad_maximum_fusion.1
  21.8 4.8 %collective-permute-start.1 = (bf16[2,256,256]{2,1,0:T(8,128)(2,1)S(1)}, bf16[2,256,256]{2,1,0:T(8,128)(2,1)S(1)}, u32[]{:S(2)}, u32[]{:S(2)}) collective-permute-start(bf16[2,256,256]{2,1,0:T(8,128)(2,1)S(1)} %pad_maximum_fusion.1), channel_id=1, source_target_pairs={{0,128},{32,416},{64,192},{96,480},{128,256},{160,32},{192,320},{2... | collective-permute-start | bytes 786440 | tf_op jit(solution)/shard_map/ppermute | solution.py:249
  26.6 6.8 %all-to-all-done.in_ref = f32[32,16,128]{2,1,0:T(8,128)S(1)} async-done(((f32[32,16,128]{2,1,0:T(8,128)}), f32[32,16,128]{2,1,0:T(8,128)S(1)}, u32[]{:S(2)}, u32[]{:S(2)}) %all-to-all-start) | async-done | bytes 262176 | tf_op jit(solution)/shard_map/all_to_all | solution.py:250
  33.4 0.7 prefix.1.refs_0_
  34.2 0.1 pad_maximum_fusion.refs_0_
  34.2 5.6 %collective-permute-start.3 = (bf16[4,256,256]{2,1,0:T(8,128)(2,1)S(1)}, bf16[4,256,256]{2,1,0:T(8,128)(2,1)}, u32[]{:S(2)}, u32[]{:S(2)}) collective-permute-start(bf16[4,256,256]{2,1,0:T(8,128)(2,1)S(1)} %pad_maximum_fusion.refs_0_), channel_id=1, source_target_pairs={{0,64},{32,480},{64,128},{96,32},{128,192},{160,96},{192,256},{224... | collective-permute-start | bytes 1572872 | tf_op jit(solution)/shard_map/ppermute | solution.py:255
  39.8 9.8 %all-to-all-start.1 = ((f32[32,8,128]{2,1,0:T(8,128)}), f32[32,8,128]{2,1,0:T(8,128)S(1)}, u32[]{:S(2)}, u32[]{:S(2)}) async-start(f32[32,8,128]{2,1,0:T(8,128)} %prefix.1.refs_0_), calls=%async_computation.1 | async-start | bytes 262144 | tf_op jit(solution)/shard_map/all_to_all | solution.py:258
  49.6 0.5 within.1.within_ref.refs_1_
  50.1 1.9 %collective-permute-start.2 = (bf16[4,256,256]{2,1,0:T(8,128)(2,1)S(1)}, bf16[4,256,256]{2,1,0:T(8,128)(2,1)}, u32[]{:S(2)}, u32[]{:S(2)}) collective-permute-start(bf16[4,256,256]{2,1,0:T(8,128)(2,1)S(1)} %pad_maximum_fusion.refs_0_), channel_id=1, source_target_pairs={{0,32},{32,0},{64,96},{96,64},{128,160},{160,128},{192,224},{224,1... | collective-permute-start | bytes 1572872 | tf_op jit(solution)/shard_map/ppermute | solution.py:257
  52.0 8.0 %all-to-all-done.1 = f32[32,8,128]{2,1,0:T(8,128)S(1)} async-done(((f32[32,8,128]{2,1,0:T(8,128)}), f32[32,8,128]{2,1,0:T(8,128)S(1)}, u32[]{:S(2)}, u32[]{:S(2)}) %all-to-all-start.1) | async-done | bytes 131104 | tf_op jit(solution)/shard_map/all_to_all | solution.py:258
  60.1 1.9 %collective-permute-start.4 = (bf16[4,256,256]{2,1,0:T(8,128)(2,1)}, bf16[4,256,256]{2,1,0:T(8,128)(2,1)}, u32[]{:S(2)}, u32[]{:S(2)}) collective-permute-start(bf16[4,256,256]{2,1,0:T(8,128)(2,1)} %gate.3.refs_2_), channel_id=1, source_target_pairs={{0,32},{32,0},{64,96},{96,64},{128,160},{160,128},{192,224},{224,1... | collective-permute-start | bytes 1572872 | tf_op jit(solution)/shard_map/ppermute | solution.py:261
  62.0 0.1 pad_add_fusion.place_ref
  62.1 1.0 forward.1
  63.1 1.1 %collective-permute-done.4.refs_3_ = bf16[4,256,256]{2,1,0:T(8,128)(2,1)} collective-permute-done((bf16[4,256,256]{2,1,0:T(8,128)(2,1)}, bf16[4,256,256]{2,1,0:T(8,128)(2,1)}, u32[]{:S(2)}, u32[]{:S(2)}) %collective-permute-start.4) | collective-permute-done | bytes 524320 | tf_op jit(solution)/shard_map/ppermute | solution.py:261
  64.2 3.2 %cotangent.1 = (f32[32,16,128]{2,1,0:T(8,128)S(1)}, bf16[256,256]{1,0:T(8,128)(2,1)S(1)}, bf16[256,256]{1,0:T(8,128)(2,1)S(1)}) custom-call(s32[2]{0:T(128)S(1)} %pad_add_fusion.place_ref, bf16[4,256,256]{2,1,0:T(8,128)(2,1)S(1)} %pad_maximum_fusion.refs_0_, bf16[4,256,256]{2,1,0:T(8,128)(2,1)} %collective-permute-done.2.refs_1_, ...), custom_call_target="tpu_custom_call" | custom-call | bytes 11070000 | tf_op jit(solution)/shard_map/cotangent/pallas_call | solution.py:188
  67.5 16.6 %all_to_all.20.in_ref = f32[32,16,128]{2,1,0:T(8,128)S(1)} all-to-all(f32[32,16,128]{2,1,0:T(8,128)S(1)} %get-tuple-element.26), channel_id=1, replica_groups=mesh['heads'=16,'seq'=32] {'seq'}, dimensions={0} | all-to-all | bytes 524288 | tf_op jit(solution)/shard_map/all_to_all | solution.py:278
  84.1 0.7 suffix.1
  84.9 3.9 %all-to-all-start.3 = ((f32[32,16,128]{2,1,0:T(8,128)}), f32[32,16,128]{2,1,0:T(8,128)S(1)}, u32[]{:S(2)}, u32[]{:S(2)}) async-start(f32[32,16,128]{2,1,0:T(8,128)} %get-tuple-element.27), calls=%async_computation.3 | async-start | bytes 524288 | tf_op jit(solution)/shard_map/all_to_all | solution.py:296
  88.7 1.8 %local.1 = (bf16[256,256]{1,0:T(8,128)(2,1)}, f32[256,256]{1,0:T(8,128)S(1)}, f32[256,256]{1,0:T(8,128)S(1)}) custom-call(bf16[256,256]{1,0:T(8,128)(2,1)S(1)} %copy-done.2, bf16[256,256]{1,0:T(8,128)(2,1)S(1)} %copy-done, bf16[256,256]{1,0:T(8,128)(2,1)S(1)} %copy-done.1, f32[256,128]{1,0:T(8,128)S(1)} %bitcast.8, ...), custom_call_target="tpu_custom_call" | custom-call | bytes 11070000 | tf_op jit(solution)/shard_map/local/pallas_call | solution.py:188
  90.5 10.6 %all-to-all-done.3.s_ref = f32[32,16,128]{2,1,0:T(8,128)S(1)} async-done(((f32[32,16,128]{2,1,0:T(8,128)}), f32[32,16,128]{2,1,0:T(8,128)S(1)}, u32[]{:S(2)}, u32[]{:S(2)}) %all-to-all-start.3) | async-done | bytes 262176 | tf_op jit(solution)/shard_map/all_to_all | solution.py:296
  101.1 1.1 %final.1 = (bf16[256,256]{1,0:T(8,128)(2,1)}, bf16[256,256]{1,0:T(8,128)(2,1)}, bf16[128,256]{1,0:T(8,128)(2,1)}, bf16[128,256]{1,0:T(8,128)(2,1)}) custom-call(bf16[256,256]{1,0:T(8,128)(2,1)S(1)} %copy-done, bf16[256,256]{1,0:T(8,128)(2,1)S(1)} %copy-done.1, bf16[128,256]{1,0:T(8,128)(2,1)S(1)} %copy-done.4, bf16[128,256]{1,0:T(8,128)(2,1)S(1)} %copy-done.5, ...), custom_call_target="tpu_custom_call" | custom-call | bytes 1845000 | tf_op jit(solution)/shard_map/final/pallas_call | solution.py:188
  (22 shorter events, 0.1 us)
Async XLA Ops:
  0.6 33.5 %copy-start.7 = (bf16[256,256]{1,0:T(8,128)(2,1)S(1)}, bf16[256,256]{1,0:T(8,128)(2,1)}, u32[]{:S(2)}) copy-start(bf16[256,256]{1,0:T(8,128)(2,1)} %param.15) | copy-start | bytes 393220
  0.6 49.0 %copy-start.1 = (bf16[256,256]{1,0:T(8,128)(2,1)S(1)}, bf16[256,256]{1,0:T(8,128)(2,1)}, u32[]{:S(2)}) copy-start(bf16[256,256]{1,0:T(8,128)(2,1)} %v_ref.5) | copy-start | bytes 393220
  0.7 49.0 %copy-start = (bf16[256,256]{1,0:T(8,128)(2,1)S(1)}, bf16[256,256]{1,0:T(8,128)(2,1)}, u32[]{:S(2)}) copy-start(bf16[256,256]{1,0:T(8,128)(2,1)} %k_ref.5) | copy-start | bytes 393220
  0.7 49.0 %copy-start.2 = (bf16[256,256]{1,0:T(8,128)(2,1)S(1)}, bf16[256,256]{1,0:T(8,128)(2,1)}, u32[]{:S(2)}) copy-start(bf16[256,256]{1,0:T(8,128)(2,1)} %q_ref.5) | copy-start | bytes 393220
  0.7 20.2 %collective-permute-start = (bf16[1,256,256]{2,1,0:T(8,128)(2,1)}, bf16[1,256,256]{2,1,0:T(8,128)(2,1)S(1)}, u32[]{:S(2)}, u32[]{:S(2)}) collective-permute-start(bf16[1,256,256]{2,1,0:T(8,128)(2,1)} %bitcast.11), channel_id=1, source_target_pairs={{0,256},{32,288},{64,320},{96,352},{128,384},{160,416},{192,448},{... | collective-permute-start | bytes 393224 | tf_op jit(solution)/shard_map/ppermute | solution.py:238
  7.7 25.8 %all-to-all-start = ((f32[32,16,128]{2,1,0:T(8,128)}), f32[32,16,128]{2,1,0:T(8,128)S(1)}, u32[]{:S(2)}, u32[]{:S(2)}) async-start(f32[32,16,128]{2,1,0:T(8,128)} %states.1), calls=%async_computation | async-start | bytes 524288 | tf_op jit(solution)/shard_map/all_to_all | solution.py:250
  21.8 12.4 %collective-permute-start.1 = (bf16[2,256,256]{2,1,0:T(8,128)(2,1)S(1)}, bf16[2,256,256]{2,1,0:T(8,128)(2,1)S(1)}, u32[]{:S(2)}, u32[]{:S(2)}) collective-permute-start(bf16[2,256,256]{2,1,0:T(8,128)(2,1)S(1)} %pad_maximum_fusion.1), channel_id=1, source_target_pairs={{0,128},{32,416},{64,192},{96,480},{128,256},{160,32},{192,320},{2... | collective-permute-start | bytes 786440 | tf_op jit(solution)/shard_map/ppermute | solution.py:249
  34.1 28.0 %copy-start.6 = (f32[256]{0:T(256)S(1)}, f32[256]{0:T(256)}, u32[]{:S(2)}) copy-start(f32[256]{0:T(256)} %param.13) | copy-start | bytes 3076
  34.2 30.1 %copy-start.3 = (bf16[256,4096]{1,0:T(8,128)(2,1)S(1)}, bf16[256,4096]{1,0:T(8,128)(2,1)}, u32[]{:S(2)}) copy-start(bf16[256,4096]{1,0:T(8,128)(2,1)} %refs_4_.1) | copy-start | bytes 6291460
  34.2 25.9 %collective-permute-start.3 = (bf16[4,256,256]{2,1,0:T(8,128)(2,1)S(1)}, bf16[4,256,256]{2,1,0:T(8,128)(2,1)}, u32[]{:S(2)}, u32[]{:S(2)}) collective-permute-start(bf16[4,256,256]{2,1,0:T(8,128)(2,1)S(1)} %pad_maximum_fusion.refs_0_), channel_id=1, source_target_pairs={{0,64},{32,480},{64,128},{96,32},{128,192},{160,96},{192,256},{224... | collective-permute-start | bytes 1572872 | tf_op jit(solution)/shard_map/ppermute | solution.py:255
  39.8 20.3 %all-to-all-start.1 = ((f32[32,8,128]{2,1,0:T(8,128)}), f32[32,8,128]{2,1,0:T(8,128)S(1)}, u32[]{:S(2)}, u32[]{:S(2)}) async-start(f32[32,8,128]{2,1,0:T(8,128)} %prefix.1.refs_0_), calls=%async_computation.1 | async-start | bytes 262144 | tf_op jit(solution)/shard_map/all_to_all | solution.py:258
  50.1 13.0 %collective-permute-start.2 = (bf16[4,256,256]{2,1,0:T(8,128)(2,1)S(1)}, bf16[4,256,256]{2,1,0:T(8,128)(2,1)}, u32[]{:S(2)}, u32[]{:S(2)}) collective-permute-start(bf16[4,256,256]{2,1,0:T(8,128)(2,1)S(1)} %pad_maximum_fusion.refs_0_), channel_id=1, source_target_pairs={{0,32},{32,0},{64,96},{96,64},{128,160},{160,128},{192,224},{224,1... | collective-permute-start | bytes 1572872 | tf_op jit(solution)/shard_map/ppermute | solution.py:257
  60.1 4.1 %collective-permute-start.4 = (bf16[4,256,256]{2,1,0:T(8,128)(2,1)}, bf16[4,256,256]{2,1,0:T(8,128)(2,1)}, u32[]{:S(2)}, u32[]{:S(2)}) collective-permute-start(bf16[4,256,256]{2,1,0:T(8,128)(2,1)} %gate.3.refs_2_), channel_id=1, source_target_pairs={{0,32},{32,0},{64,96},{96,64},{128,160},{160,128},{192,224},{224,1... | collective-permute-start | bytes 1572872 | tf_op jit(solution)/shard_map/ppermute | solution.py:261
  67.4 33.6 %copy-start.4 = (bf16[128,256]{1,0:T(8,128)(2,1)S(1)}, bf16[128,256]{1,0:T(8,128)(2,1)}, u32[]{:S(2)}) copy-start(bf16[128,256]{1,0:T(8,128)(2,1)} %sk_ref.1) | copy-start | bytes 196612
  67.5 33.6 %copy-start.5 = (bf16[128,256]{1,0:T(8,128)(2,1)S(1)}, bf16[128,256]{1,0:T(8,128)(2,1)}, u32[]{:S(2)}) copy-start(bf16[128,256]{1,0:T(8,128)(2,1)} %sv_ref.1) | copy-start | bytes 196612
  84.9 16.2 %all-to-all-start.3 = ((f32[32,16,128]{2,1,0:T(8,128)}), f32[32,16,128]{2,1,0:T(8,128)S(1)}, u32[]{:S(2)}, u32[]{:S(2)}) async-start(f32[32,16,128]{2,1,0:T(8,128)} %get-tuple-element.27), calls=%async_computation.3 | async-start | bytes 524288 | tf_op jit(solution)/shard_map/all_to_all | solution.py:296

commit v3 on v2

--- a/solution.py
+++ b/solution.py
@@ -73,7 +73,7 @@
     return causal, halves(jnp.where(causal, dot(q, k, 1, 1), 0.0) * self_scale)
 
 
-def within_kernel(q_ref, k_ref, v_ref, out_ref, *, heads, self_scale):
+def within_kernel(q_ref, k_ref, v_ref, _, out_ref, *, heads, self_scale):
     for h in range(heads):
         v = v_ref[:, head(h)]
         _, (high, low) = masked_scores(q_ref[:, head(h)], k_ref[:, head(h)], self_scale)
@@ -178,7 +178,7 @@
 HBM = pl.BlockSpec(memory_space=pltpu.HBM)
 
 
-MICROSECONDS = {"states": 10, "pack": 10, "within": 20, "forward": 2, "cotangent": 3, "local": 3}
+MICROSECONDS = {"states": 40, "pack": 40, "within": 40, "forward": 40, "cotangent": 3, "local": 3}
 
 
 def call(kernel, outs, name, ins=None, scratch=(), aliases=None, out_specs=None, **static):
@@ -194,7 +194,7 @@
             input_output_aliases=aliases or {},
             compiler_params=pltpu.CompilerParams(vmem_limit_bytes=12 * MIB),
             name=name,
-            cost_estimate=pl.CostEstimate(flops=0, transcendentals=0, bytes_accessed=int(MICROSECONDS.get(name, 0.5) * 3.69e6)),
+            cost_estimate=pl.CostEstimate(flops=int(MICROSECONDS.get(name, 0.5) * 1e9), transcendentals=0, bytes_accessed=int(MICROSECONDS.get(name, 0.5) * 3.69e6)),
         )(*operands)
 
     return run
@@ -245,26 +245,26 @@
         heads=heads,
         rows=rows,
     )(*(pltpu.with_memory_space_constraint(x, pltpu.HBM) for x in (keys, values, src_keys, src_values)))
-    held = jnp.concatenate([grad_out[None], across], axis=0)
-    held_next = lax.ppermute(held, "heads", along(2))
+    held = pack([grad_out[None], across], grad_out)
+    second, above, below = (lax.ppermute(held, "heads", along(d)) for d in (2, 1, -1))
     own = lax.all_to_all(own, "seq", 0, 0)
     (before,) = call(
         prefix_kernel, [((count, rows, DH), f32)], "prefix", count=count, rows=rows, self_scale=self_scale, cross_scale=cross_scale
     )(own)
-    held = jnp.concatenate([held, gate(held_next, before)], axis=0)
-    got = lax.ppermute(held, "heads", along(1))
+    (within,) = call(
+        within_kernel, [((length, width), f32)], "within", ins=[WHOLE] * 3 + [ANY], heads=heads, self_scale=self_scale
+    )(queries, keys, values, before)
+    second, above, below = (gate(x, within) for x in (second, above, below))
     swap = [(i, i ^ 1) for i in range(groups)]
-    other_held = lax.ppermute(held, "heads", swap)
+    even = jnp.concatenate([held, second], axis=0)
+    odd = jnp.concatenate([above, below], axis=0)
+    other_even, other_odd = (lax.ppermute(x, "heads", swap) for x in (even, odd))
     before = lax.all_to_all(before, "seq", 0, 0).reshape(width, DH)
-    (within,) = call(within_kernel, [((length, width), f32)], "within", heads=heads, self_scale=self_scale)(queries, keys, values)
-    got = gate(got, before, within)
-    other_got = lax.ppermute(got, "heads", swap)
     attended, mixture = call(forward_kernel, [((length, width), bf16), ((length, width), f32)], "forward", heads=heads)(
         queries, within, before, gain
     )
-    blocks = [held, other_held, got, other_got]
-    quad = [(0, None), (4, None), (2, None), (6, None)]
-    parts = [[((d + far) % chips, swapped, None) for d, _ in quad] for far in (0, 1) for swapped in (False, True)]
+    blocks = [even, odd, other_even, other_odd]
+    parts = [[(d, swapped, None) for d in steps] for swapped in (False, True) for steps in ((0, 4, 2, 6), (1, 5, 7, 3))]
     outer, g_high, g_low = call(
         cotangent_kernel,
         [((count, 2 * rows, DH), f32), ((length, width), bf16), ((length, width), bf16)],

time: 103 us -> 94.7 us (0.919)
  the two profiles are of different devices: /device:TPU:56 before, /device:TPU:8 now
where the time goes in v3:
time: 94.7 us; the launch traced here: 94.1 us
  starting transfers between devices  45.8 us (48%)
  waiting for transfers between devices  18.2 us (19%)
  blocking collectives  17.5 us (18%)
  Pallas kernels  10.9 us (12%)
    all_to_all x1, blocking collectives, on_device(): outer = lax.all_to_all(outer, 'seq', 0, 0)  17.5 us
    all_to_all x1, starting transfers between devices, on_device(): own = lax.all_to_all(own, 'seq', 0, 0)  13.2 us
    pallas_call x12, Pallas kernels, run(): pl.pallas_call(functools.partial(kernel, **static), out_shape=shapes, in_...  10.9 us
    all_to_all x1, waiting for transfers between devices, on_device(): later = lax.all_to_all(later, 'seq', 0, 0)  10.5 us
    ppermute x3, starting transfers between devices, on_device(): lax.ppermute(held, 'heads', along(d))  9.89 us
    all_to_all x1, starting transfers between devices, on_device(): before = lax.all_to_all(before, 'seq', 0, 0).reshape(width, DH)  7.61 us
    ppermute x1, starting transfers between devices, on_device(): across = lax.ppermute(grad_out[None], 'heads', along(chips // 2))  6.97 us
    all_to_all x1, waiting for transfers between devices, on_device(): before = lax.all_to_all(before, 'seq', 0, 0).reshape(width, DH)  5.49 us
  transfers between devices with their start and end apart: 9, of which 3 were waited for; matrix products, arithmetic and copies ran while one was open for 0% of the time, Pallas kernels for 7%

profile of v3, /device:TPU:8, one launch (start us, length us, event | category | flops | bytes accessed | tf_op | source)
XLA Modules:
  0.0 94.1 jit_solution(13625787034477684486)
XLA Ops:
  0.6 7.0 %collective-permute-start = (bf16[1,256,256]{2,1,0:T(8,128)(2,1)}, bf16[1,256,256]{2,1,0:T(8,128)(2,1)S(1)}, u32[]{:S(2)}, u32[]{:S(2)}) collective-permute-start(bf16[1,256,256]{2,1,0:T(8,128)(2,1)} %bitcast.8), channel_id=1, source_target_pairs={{0,256},{32,288},{64,320},{96,352},{128,384},{160,416},{192,448},{... | collective-permute-start | bytes 393224 | tf_op jit(solution)/shard_map/ppermute | solution.py:238
  7.6 2.1 %states.1 = f32[32,16,128]{2,1,0:T(8,128)} custom-call(bf16[256,256]{1,0:T(8,128)(2,1)} %k_ref.5, bf16[256,256]{1,0:T(8,128)(2,1)} %v_ref.5, bf16[128,256]{1,0:T(8,128)(2,1)} %sk_ref.1, bf16[128,256]{1,0:T(8,128)(2,1)} %sv_ref.1), custom_call_target="tpu_custom_call" | custom-call | flops 40000000000 | bytes 147600000 | tf_op jit(solution)/shard_map/states/pallas_call | solution.py:188
  9.8 13.2 %all-to-all-start = ((f32[32,16,128]{2,1,0:T(8,128)}), f32[32,16,128]{2,1,0:T(8,128)S(1)}, u32[]{:S(2)}, u32[]{:S(2)}) async-start(f32[32,16,128]{2,1,0:T(8,128)} %states.1), calls=%async_computation | async-start | bytes 524288 | tf_op jit(solution)/shard_map/all_to_all | solution.py:250
  23.0 0.1 pad_add_fusion.place_ref
  23.1 0.3 pack.1
  23.4 3.4 %collective-permute-start.3 = (bf16[2,256,256]{2,1,0:T(8,128)(2,1)S(1)}, bf16[2,256,256]{2,1,0:T(8,128)(2,1)S(1)}, u32[]{:S(2)}, u32[]{:S(2)}) collective-permute-start(bf16[2,256,256]{2,1,0:T(8,128)(2,1)S(1)} %pack.1), channel_id=1, source_target_pairs={{0,448},{32,96},{64,0},{96,160},{128,64},{160,224},{192,128},{224,... | collective-permute-start | bytes 786440 | tf_op jit(solution)/shard_map/ppermute | solution.py:249
  26.8 2.6 %collective-permute-start.2 = (bf16[2,256,256]{2,1,0:T(8,128)(2,1)S(1)}, bf16[2,256,256]{2,1,0:T(8,128)(2,1)S(1)}, u32[]{:S(2)}, u32[]{:S(2)}) collective-permute-start(bf16[2,256,256]{2,1,0:T(8,128)(2,1)S(1)} %pack.1), channel_id=1, source_target_pairs={{0,64},{32,480},{64,128},{96,32},{128,192},{160,96},{192,256},{224... | collective-permute-start | bytes 786440 | tf_op jit(solution)/shard_map/ppermute | solution.py:249
  29.4 3.9 %collective-permute-start.1 = (bf16[2,256,256]{2,1,0:T(8,128)(2,1)S(1)}, bf16[2,256,256]{2,1,0:T(8,128)(2,1)S(1)}, u32[]{:S(2)}, u32[]{:S(2)}) collective-permute-start(bf16[2,256,256]{2,1,0:T(8,128)(2,1)S(1)} %pack.1), channel_id=1, source_target_pairs={{0,128},{32,416},{64,192},{96,480},{128,256},{160,32},{192,320},{2... | collective-permute-start | bytes 786440 | tf_op jit(solution)/shard_map/ppermute | solution.py:249
  33.4 2.2 %all-to-all-done.in_ref = f32[32,16,128]{2,1,0:T(8,128)S(1)} async-done(((f32[32,16,128]{2,1,0:T(8,128)}), f32[32,16,128]{2,1,0:T(8,128)S(1)}, u32[]{:S(2)}, u32[]{:S(2)}) %all-to-all-start) | async-done | bytes 262176 | tf_op jit(solution)/shard_map/all_to_all | solution.py:250
  35.5 0.7 prefix.1._
  36.3 7.6 %all-to-all-start.1 = ((f32[32,8,128]{2,1,0:T(8,128)}), f32[32,8,128]{2,1,0:T(8,128)S(1)}, u32[]{:S(2)}, u32[]{:S(2)}) async-start(f32[32,8,128]{2,1,0:T(8,128)} %prefix.1._), calls=%async_computation.1 | async-start | bytes 262144 | tf_op jit(solution)/shard_map/all_to_all | solution.py:262
  43.9 0.5 within.1.within_ref.refs_0_
  44.5 1.9 %collective-permute-start.4 = (bf16[4,256,256]{2,1,0:T(8,128)(2,1)S(1)}, bf16[4,256,256]{2,1,0:T(8,128)(2,1)S(1)}, u32[]{:S(2)}, u32[]{:S(2)}) collective-permute-start(bf16[4,256,256]{2,1,0:T(8,128)(2,1)S(1)} %pad_maximum_fusion.refs_0_), channel_id=1, source_target_pairs={{0,32},{32,0},{64,96},{96,64},{128,160},{160,128},{192,224},{224,1... | collective-permute-start | bytes 1572872 | tf_op jit(solution)/shard_map/ppermute | solution.py:261
  46.5 2.4 %collective-permute-start.5 = (bf16[4,256,256]{2,1,0:T(8,128)(2,1)S(1)}, bf16[4,256,256]{2,1,0:T(8,128)(2,1)S(1)}, u32[]{:S(2)}, u32[]{:S(2)}) collective-permute-start(bf16[4,256,256]{2,1,0:T(8,128)(2,1)S(1)} %pad_maximum_fusion.1.refs_1_), channel_id=1, source_target_pairs={{0,32},{32,0},{64,96},{96,64},{128,160},{160,128},{192,224},{224,1... | collective-permute-start | bytes 1572872 | tf_op jit(solution)/shard_map/ppermute | solution.py:261
  48.9 5.5 %all-to-all-done.1 = f32[32,8,128]{2,1,0:T(8,128)S(1)} async-done(((f32[32,8,128]{2,1,0:T(8,128)}), f32[32,8,128]{2,1,0:T(8,128)S(1)}, u32[]{:S(2)}, u32[]{:S(2)}) %all-to-all-start.1) | async-done | bytes 131104 | tf_op jit(solution)/shard_map/all_to_all | solution.py:262
  54.4 1.0 %forward.1 = (bf16[256,256]{1,0:T(8,128)(2,1)}, f32[256,256]{1,0:T(8,128)S(1)}) custom-call(bf16[256,256]{1,0:T(8,128)(2,1)S(1)} %copy-done.2, f32[256,256]{1,0:T(8,128)S(1)} %within.1.within_ref.refs_0_, f32[256,128]{1,0:T(8,128)S(1)} %bitcast.6, f32[2,128]{1,0:T(2,128)S(1)} %bitcast.10), custom_call_target="tpu_custom_call" | custom-call | flops 40000000000 | bytes 147600000 | tf_op jit(solution)/shard_map/forward/pallas_call | solution.py:188
  55.4 0.6 copy-done
  56.1 2.6 %cotangent.1 = (f32[32,16,128]{2,1,0:T(8,128)S(1)}, bf16[256,256]{1,0:T(8,128)(2,1)S(1)}, bf16[256,256]{1,0:T(8,128)(2,1)S(1)}) custom-call(s32[2]{0:T(128)S(1)} %pad_add_fusion.place_ref, bf16[4,256,256]{2,1,0:T(8,128)(2,1)S(1)} %pad_maximum_fusion.refs_0_, bf16[4,256,256]{2,1,0:T(8,128)(2,1)S(1)} %pad_maximum_fusion.1.refs_1_, ...), custom_call_target="tpu_custom_call" | custom-call | flops 3000000000 | bytes 11070000 | tf_op jit(solution)/shard_map/cotangent/pallas_call | solution.py:188
  58.7 17.5 %all_to_all.20.in_ref = f32[32,16,128]{2,1,0:T(8,128)S(1)} all-to-all(f32[32,16,128]{2,1,0:T(8,128)S(1)} %get-tuple-element.26), channel_id=1, replica_groups=mesh['heads'=16,'seq'=32] {'seq'}, dimensions={0} | all-to-all | bytes 524288 | tf_op jit(solution)/shard_map/all_to_all | solution.py:278
  76.1 0.8 suffix.1
  76.9 3.9 %all-to-all-start.3 = ((f32[32,16,128]{2,1,0:T(8,128)}), f32[32,16,128]{2,1,0:T(8,128)S(1)}, u32[]{:S(2)}, u32[]{:S(2)}) async-start(f32[32,16,128]{2,1,0:T(8,128)} %get-tuple-element.27), calls=%async_computation.3 | async-start | bytes 524288 | tf_op jit(solution)/shard_map/all_to_all | solution.py:296
  80.8 1.8 %local.1 = (bf16[256,256]{1,0:T(8,128)(2,1)}, f32[256,256]{1,0:T(8,128)S(1)}, f32[256,256]{1,0:T(8,128)S(1)}) custom-call(bf16[256,256]{1,0:T(8,128)(2,1)S(1)} %copy-done.2, bf16[256,256]{1,0:T(8,128)(2,1)S(1)} %copy-done.3, bf16[256,256]{1,0:T(8,128)(2,1)S(1)} %copy-done.4, f32[256,128]{1,0:T(8,128)S(1)} %bitcast.7, ...), custom_call_target="tpu_custom_call" | custom-call | flops 3000000000 | bytes 11070000 | tf_op jit(solution)/shard_map/local/pallas_call | solution.py:188
  82.6 10.5 %all-to-all-done.3.s_ref = f32[32,16,128]{2,1,0:T(8,128)S(1)} async-done(((f32[32,16,128]{2,1,0:T(8,128)}), f32[32,16,128]{2,1,0:T(8,128)S(1)}, u32[]{:S(2)}, u32[]{:S(2)}) %all-to-all-start.3) | async-done | bytes 262176 | tf_op jit(solution)/shard_map/all_to_all | solution.py:296
  93.1 1.1 %final.1 = (bf16[256,256]{1,0:T(8,128)(2,1)}, bf16[256,256]{1,0:T(8,128)(2,1)}, bf16[128,256]{1,0:T(8,128)(2,1)}, bf16[128,256]{1,0:T(8,128)(2,1)}) custom-call(bf16[256,256]{1,0:T(8,128)(2,1)S(1)} %copy-done.3, bf16[256,256]{1,0:T(8,128)(2,1)S(1)} %copy-done.4, bf16[128,256]{1,0:T(8,128)(2,1)S(1)} %copy-done.5, bf16[128,256]{1,0:T(8,128)(2,1)S(1)} %copy-done.6, ...), custom_call_target="tpu_custom_call" | custom-call | flops 500000000 | bytes 1845000 | tf_op jit(solution)/shard_map/final/pallas_call | solution.py:188
  (26 shorter events, 0.2 us)
Async XLA Ops:
  0.6 22.4 %copy-start.1 = (bf16[256,256]{1,0:T(8,128)(2,1)S(1)}, bf16[256,256]{1,0:T(8,128)(2,1)}, u32[]{:S(2)}) copy-start(bf16[256,256]{1,0:T(8,128)(2,1)} %refs_2_.1) | copy-start | bytes 393220
  0.6 22.4 %collective-permute-start = (bf16[1,256,256]{2,1,0:T(8,128)(2,1)}, bf16[1,256,256]{2,1,0:T(8,128)(2,1)S(1)}, u32[]{:S(2)}, u32[]{:S(2)}) collective-permute-start(bf16[1,256,256]{2,1,0:T(8,128)(2,1)} %bitcast.8), channel_id=1, source_target_pairs={{0,256},{32,288},{64,320},{96,352},{128,384},{160,416},{192,448},{... | collective-permute-start | bytes 393224 | tf_op jit(solution)/shard_map/ppermute | solution.py:238
  9.8 25.8 %all-to-all-start = ((f32[32,16,128]{2,1,0:T(8,128)}), f32[32,16,128]{2,1,0:T(8,128)S(1)}, u32[]{:S(2)}, u32[]{:S(2)}) async-start(f32[32,16,128]{2,1,0:T(8,128)} %states.1), calls=%async_computation | async-start | bytes 524288 | tf_op jit(solution)/shard_map/all_to_all | solution.py:250
  23.4 20.5 %copy-start.2 = (bf16[256,256]{1,0:T(8,128)(2,1)S(1)}, bf16[256,256]{1,0:T(8,128)(2,1)}, u32[]{:S(2)}) copy-start(bf16[256,256]{1,0:T(8,128)(2,1)} %q_ref.5) | copy-start | bytes 393220
  23.4 20.5 %copy-start.3 = (bf16[256,256]{1,0:T(8,128)(2,1)S(1)}, bf16[256,256]{1,0:T(8,128)(2,1)}, u32[]{:S(2)}) copy-start(bf16[256,256]{1,0:T(8,128)(2,1)} %k_ref.5) | copy-start | bytes 393220
  23.4 20.5 %copy-start.4 = (bf16[256,256]{1,0:T(8,128)(2,1)S(1)}, bf16[256,256]{1,0:T(8,128)(2,1)}, u32[]{:S(2)}) copy-start(bf16[256,256]{1,0:T(8,128)(2,1)} %v_ref.5) | copy-start | bytes 393220
  23.4 23.0 %collective-permute-start.3 = (bf16[2,256,256]{2,1,0:T(8,128)(2,1)S(1)}, bf16[2,256,256]{2,1,0:T(8,128)(2,1)S(1)}, u32[]{:S(2)}, u32[]{:S(2)}) collective-permute-start(bf16[2,256,256]{2,1,0:T(8,128)(2,1)S(1)} %pack.1), channel_id=1, source_target_pairs={{0,448},{32,96},{64,0},{96,160},{128,64},{160,224},{192,128},{224,... | collective-permute-start | bytes 786440 | tf_op jit(solution)/shard_map/ppermute | solution.py:249
  26.8 19.6 %collective-permute-start.2 = (bf16[2,256,256]{2,1,0:T(8,128)(2,1)S(1)}, bf16[2,256,256]{2,1,0:T(8,128)(2,1)S(1)}, u32[]{:S(2)}, u32[]{:S(2)}) collective-permute-start(bf16[2,256,256]{2,1,0:T(8,128)(2,1)S(1)} %pack.1), channel_id=1, source_target_pairs={{0,64},{32,480},{64,128},{96,32},{128,192},{160,96},{192,256},{224... | collective-permute-start | bytes 786440 | tf_op jit(solution)/shard_map/ppermute | solution.py:249
  29.4 15.0 %collective-permute-start.1 = (bf16[2,256,256]{2,1,0:T(8,128)(2,1)S(1)}, bf16[2,256,256]{2,1,0:T(8,128)(2,1)S(1)}, u32[]{:S(2)}, u32[]{:S(2)}) collective-permute-start(bf16[2,256,256]{2,1,0:T(8,128)(2,1)S(1)} %pack.1), channel_id=1, source_target_pairs={{0,128},{32,416},{64,192},{96,480},{128,256},{160,32},{192,320},{2... | collective-permute-start | bytes 786440 | tf_op jit(solution)/shard_map/ppermute | solution.py:249
  36.3 18.2 %all-to-all-start.1 = ((f32[32,8,128]{2,1,0:T(8,128)}), f32[32,8,128]{2,1,0:T(8,128)S(1)}, u32[]{:S(2)}, u32[]{:S(2)}) async-start(f32[32,8,128]{2,1,0:T(8,128)} %prefix.1._), calls=%async_computation.1 | async-start | bytes 262144 | tf_op jit(solution)/shard_map/all_to_all | solution.py:262
  44.5 9.9 %copy-start.7 = (f32[256]{0:T(256)S(1)}, f32[256]{0:T(256)}, u32[]{:S(2)}) copy-start(f32[256]{0:T(256)} %param.13) | copy-start | bytes 3076
  44.5 10.9 %collective-permute-start.4 = (bf16[4,256,256]{2,1,0:T(8,128)(2,1)S(1)}, bf16[4,256,256]{2,1,0:T(8,128)(2,1)S(1)}, u32[]{:S(2)}, u32[]{:S(2)}) collective-permute-start(bf16[4,256,256]{2,1,0:T(8,128)(2,1)S(1)} %pad_maximum_fusion.refs_0_), channel_id=1, source_target_pairs={{0,32},{32,0},{64,96},{96,64},{128,160},{160,128},{192,224},{224,1... | collective-permute-start | bytes 1572872 | tf_op jit(solution)/shard_map/ppermute | solution.py:261
  46.5 8.9 %collective-permute-start.5 = (bf16[4,256,256]{2,1,0:T(8,128)(2,1)S(1)}, bf16[4,256,256]{2,1,0:T(8,128)(2,1)S(1)}, u32[]{:S(2)}, u32[]{:S(2)}) collective-permute-start(bf16[4,256,256]{2,1,0:T(8,128)(2,1)S(1)} %pad_maximum_fusion.1.refs_1_), channel_id=1, source_target_pairs={{0,32},{32,0},{64,96},{96,64},{128,160},{160,128},{192,224},{224,1... | collective-permute-start | bytes 1572872 | tf_op jit(solution)/shard_map/ppermute | solution.py:261
  54.4 1.6 %copy-start = (bf16[256,4096]{1,0:T(8,128)(2,1)S(1)}, bf16[256,4096]{1,0:T(8,128)(2,1)}, u32[]{:S(2)}) copy-start(bf16[256,4096]{1,0:T(8,128)(2,1)} %refs_4_.1) | copy-start | bytes 6291460
  76.9 16.2 %all-to-all-start.3 = ((f32[32,16,128]{2,1,0:T(8,128)}), f32[32,16,128]{2,1,0:T(8,128)S(1)}, u32[]{:S(2)}, u32[]{:S(2)}) async-start(f32[32,16,128]{2,1,0:T(8,128)} %get-tuple-element.27), calls=%async_computation.3 | async-start | bytes 524288 | tf_op jit(solution)/shard_map/all_to_all | solution.py:296
  80.8 12.3 %copy-start.5 = (bf16[128,256]{1,0:T(8,128)(2,1)S(1)}, bf16[128,256]{1,0:T(8,128)(2,1)}, u32[]{:S(2)}) copy-start(bf16[128,256]{1,0:T(8,128)(2,1)} %sk_ref.1) | copy-start | bytes 196612
  80.8 12.3 %copy-start.6 = (bf16[128,256]{1,0:T(8,128)(2,1)S(1)}, bf16[128,256]{1,0:T(8,128)(2,1)}, u32[]{:S(2)}) copy-start(bf16[128,256]{1,0:T(8,128)(2,1)} %sv_ref.1) | copy-start | bytes 196612

commit v4 on v3

--- a/solution.py
+++ b/solution.py
@@ -80,29 +80,22 @@
         out_ref[:, head(h)] = dot(high, v, 1, 0) + dot(low, v, 1, 0)
 
 
-def forward_kernel(q_ref, within_ref, c_ref, gain_ref, att_ref, mix_ref, *, heads):
+def forward_kernel(q_ref, within_ref, c_ref, mix_ref, *, heads):
     for h in range(heads):
         q = q_ref[:, head(h)]
         c_high, c_low = halves(c_ref[head(h), :])
         mixture = within_ref[:, head(h)] + dot(q, c_high, 1, 0) + dot(q, c_low, 1, 0)
         mix_ref[:, head(h)] = mixture
-        inverse = lax.rsqrt(jnp.mean(mixture * mixture, axis=-1, keepdims=True) + 1e-06)
-        att_ref[:, head(h)] = (mixture * inverse * gain_ref[h : h + 1, :]).astype(bf16)
 
 
 def cotangent_kernel(place_ref, *refs, heads, rows, parts):
-    blocks = refs[: len(parts)]
-    w_ref, q_ref, mix_ref, gain_ref, out_ref, high_ref, low_ref = refs[len(parts) : len(parts) + 7]
-    held, sems = refs[len(parts) + 7 : -1], refs[-1]
-    loads = [pltpu.make_async_copy(a, b, sems.at[i]) for i, (a, b) in enumerate(zip(blocks, held))]
-    for load in loads:
-        load.start()
+    held = refs[: len(parts)]
+    w_ref, q_ref, mix_ref, gain_ref, out_ref, high_ref, low_ref = refs[len(parts) :]
     length, width = held[0].shape[1:]
     chip, core = place_ref[0], place_ref[1]
     chips = w_ref.shape[1] // (2 * width)
     grad_normed = jnp.zeros((length, width), f32)
-    for load, ref, part in zip(loads, held, parts):
-        load.wait()
+    for ref, part in zip(held, parts):
         for b, (steps, swapped, which) in enumerate(part):
             side = 1 - core if swapped else core
             source = lax.rem(chip + chips + (2 * side - 1) * steps, chips)
@@ -124,13 +117,19 @@
         low_ref[:, head(h)] = low
         q = q_ref[:, head(h)]
         outer = dot(q, high, 0, 0) + dot(q, low, 0, 0)
-        out_ref[h * per : (h + 1) * per, :rows, :] = outer.reshape(per, rows, DH)
-    gain = jnp.concatenate(gains + [jnp.zeros((rows - heads, DH), f32)], axis=0)
-    out_ref[:, rows:, :] = jnp.broadcast_to(gain[None], (heads * per, rows, DH))
-
-
-def local_kernel(q_ref, k_ref, v_ref, c_ref, gh_ref, gl_ref, gq_ref, gk_ref, gv_ref, *, heads, self_scale):
-    for h in range(heads):
+        for at in range(0, DH, heads):
+            out_ref[h * per + at // rows, at % rows // heads] = outer[at : at + heads, :]
+    gain = jnp.concatenate(gains, axis=0)
+    out_ref[:, rows // heads] = jnp.broadcast_to(gain[None], (heads * per, heads, DH))
+
+
+def local_kernel(
+    q_ref, k_ref, v_ref, c_ref, mix_ref, gain_ref, gh_ref, gl_ref, att_ref, gq_ref, gk_ref, gv_ref, *, heads, self_scale
+):
+    for h in range(heads):
+        mixture = mix_ref[:, head(h)]
+        inverse = lax.rsqrt(jnp.mean(mixture * mixture, axis=-1, keepdims=True) + 1e-06)
+        att_ref[:, head(h)] = (mixture * inverse * gain_ref[h : h + 1, :]).astype(bf16)
         q, k, v = q_ref[:, head(h)], k_ref[:, head(h)], v_ref[:, head(h)]
         high, low = gh_ref[:, head(h)], gl_ref[:, head(h)]
         causal, (m_high, m_low) = masked_scores(q, k, self_scale)
@@ -145,17 +144,20 @@
 
 
 def suffix_kernel(in_ref, out_ref, gain_ref, *, count, rows, heads, self_scale, cross_scale):
-    gain = in_ref[0, rows:, :]
+    tiles = rows // heads
+    gain = in_ref[0, tiles]
     for j in range(1, count):
-        gain = gain + in_ref[j, rows:, :]
-    gain_ref[...] = gain[:heads, :]
-    state = jnp.zeros((rows, DH), f32)
-    for j in range(count - 1, -1, -1):
-        out_ref[j, :rows, :] = state * self_scale
-        state = state + in_ref[j, :rows, :]
-    total = state * cross_scale
-    for j in range(count):
-        out_ref[j, rows:, :] = total
+        gain = gain + in_ref[j, tiles]
+    gain_ref[...] = gain
+    for tile in range(tiles):
+        at = tile * heads
+        state = jnp.zeros((heads, DH), f32)
+        for j in range(count):
+            out_ref[j, at : at + heads, :] = state * self_scale
+            state = state + in_ref[j, tile]
+        total = state * cross_scale
+        for j in range(count):
+            out_ref[j, rows + at : rows + at + heads, :] = total
 
 
 def final_kernel(k_ref, v_ref, sk_ref, sv_ref, s_ref, gk_ref, gv_ref, out_k, out_v, out_sk, out_sv, *, heads, rows):
@@ -226,6 +228,7 @@
     self_scale = 1.0 / math.sqrt(DH * length * count)
     cross_scale = 1.0 / math.sqrt(DH * src_length * count)
     gain = norm_gain.reshape(heads, DH)
+    backwards = [list(range(count - 1, -1, -1))]
 
     chips = groups // 2
     chip = lax.axis_index("heads") // 2
@@ -235,7 +238,7 @@
     def along(d):
         return [(2 * y + c, 2 * ((y + (d if c == 0 else -d)) % chips) + c) for y in range(chips) for c in range(2)]
 
-    across = lax.ppermute(grad_out[None], "heads", along(chips // 2))
+    across = lax.ppermute(grad_out[None], "heads", along(4))
     (own,) = call(
         states_kernel,
         [((count, 2 * rows, DH), f32)],
@@ -255,34 +258,29 @@
         within_kernel, [((length, width), f32)], "within", ins=[WHOLE] * 3 + [ANY], heads=heads, self_scale=self_scale
     )(queries, keys, values, before)
     second, above, below = (gate(x, within) for x in (second, above, below))
-    swap = [(i, i ^ 1) for i in range(groups)]
-    even = jnp.concatenate([held, second], axis=0)
-    odd = jnp.concatenate([above, below], axis=0)
-    other_even, other_odd = (lax.ppermute(x, "heads", swap) for x in (even, odd))
+    whole = jnp.concatenate([held, second, above, below], axis=0)
+    other = lax.ppermute(whole, "heads", [(i, i ^ 1) for i in range(groups)])
     before = lax.all_to_all(before, "seq", 0, 0).reshape(width, DH)
-    attended, mixture = call(forward_kernel, [((length, width), bf16), ((length, width), f32)], "forward", heads=heads)(
-        queries, within, before, gain
-    )
-    blocks = [even, odd, other_even, other_odd]
-    parts = [[(d, swapped, None) for d in steps] for swapped in (False, True) for steps in ((0, 4, 2, 6), (1, 5, 7, 3))]
+    (mixture,) = call(forward_kernel, [((length, width), f32)], "forward", heads=heads)(queries, within, before)
+    blocks = [whole, other]
+    parts = [[(d, swapped, None) for d in steps] for swapped in (False, True) for steps in ((0, 4, 2, 6, 1, 5, 7, 3),)]
     outer, g_high, g_low = call(
         cotangent_kernel,
-        [((count, 2 * rows, DH), f32), ((length, width), bf16), ((length, width), bf16)],
+        [((count, rows // heads + 1, heads, DH), f32), ((length, width), bf16), ((length, width), bf16)],
         "cotangent",
-        ins=[SCALAR] + [ANY] * len(blocks) + [WHOLE] * 4,
-        scratch=[pltpu.VMEM(x.shape, x.dtype) for x in blocks] + [pltpu.SemaphoreType.DMA((len(blocks),))],
+        ins=[SCALAR] + [WHOLE] * (len(blocks) + 4),
         heads=heads,
         rows=rows,
         parts=parts,
     )(place, *blocks, out_weight, queries, mixture, gain)
-    outer = lax.all_to_all(outer, "seq", 0, 0)
-    grad_query, grad_key, grad_value = call(
+    outer = lax.all_to_all(outer, "seq", 0, 0, axis_index_groups=backwards)
+    attended, grad_query, grad_key, grad_value = call(
         local_kernel,
-        [((length, width), bf16), ((length, width), f32), ((length, width), f32)],
+        [((length, width), bf16), ((length, width), bf16), ((length, width), f32), ((length, width), f32)],
         "local",
         heads=heads,
         self_scale=self_scale,
-    )(queries, keys, values, before, g_high, g_low)
+    )(queries, keys, values, before, mixture, gain, g_high, g_low)
     later, grad_gain = call(
         suffix_kernel,
         [((count, 2 * rows, DH), f32), ((heads, DH), f32)],
@@ -293,7 +291,7 @@
         self_scale=self_scale,
         cross_scale=cross_scale,
     )(outer)
-    later = lax.all_to_all(later, "seq", 0, 0)
+    later = lax.all_to_all(later, "seq", 0, 0, axis_index_groups=backwards)
     grad_key, grad_value, grad_src_key, grad_src_value = call(
         final_kernel,
         [((length, width), bf16), ((length, width), bf16), ((src_length, width), bf16), ((src_length, width), bf16)],

time: 94.7 us -> 89 us (0.940)
  blocking collectives: 17.5 us -> 13.6 us
  waiting for transfers between devices: 18.2 us -> 15.3 us
  starting transfers between devices: 45.8 us -> 47.8 us
  Pallas kernels: 10.9 us -> 9.37 us
    all_to_all x1, waiting for transfers between devices: 10.5 us -> 5.2 us  [on_device(): later = lax.all_to_all(later, 'seq', 0, 0, axis_index_groups=backwards)]
    all_to_all x1, starting transfers between devices: 3.87 us -> 8.21 us  [on_device(): later = lax.all_to_all(later, 'seq', 0, 0, axis_index_groups=backwards)]
    all_to_all x1, blocking collectives: 17.5 us -> 13.6 us  [on_device(): outer = lax.all_to_all(outer, 'seq', 0, 0, axis_index_groups=backwards)]
    ppermute x3 -> x2, starting transfers between devices: 11.3 us -> 8.89 us  [the longest x1 6.97 us: on_device(): across = lax.ppermute(grad_out[None], 'heads', along(4))]
    all_to_all x1, waiting for transfers between devices: 5.49 us -> 7.89 us  [on_device(): before = lax.all_to_all(before, 'seq', 0, 0).reshape(width, DH)]
    pallas_call x12, Pallas kernels: 10.9 us -> 9.37 us  [run(): pl.pallas_call(functools.partial(kernel, **static), out_shape=shapes, in_...]
  transfers between devices with their start and end apart: 9 -> 8, of which waited for: 3 -> 3; matrix products, arithmetic and copies ran while one was open for 0% -> 0% of each run, Pallas kernels for 7% -> 7%
where the time goes in v4:
time: 89 us; the launch traced here: 88.5 us
  starting transfers between devices  47.8 us (54%)
  waiting for transfers between devices  15.3 us (17%)
  blocking collectives  13.6 us (15%)
  Pallas kernels  9.37 us (11%)
  local copies, waits for them, and re-layouts  1.39 us (2%)
  between operations  0.89 us (1%)
    all_to_all x1, blocking collectives, on_device(): outer = lax.all_to_all(outer, 'seq', 0, 0, axis_index_groups=backwards)  13.6 us
    all_to_all x1, starting transfers between devices, on_device(): own = lax.all_to_all(own, 'seq', 0, 0)  13.2 us
    ppermute x3, starting transfers between devices, on_device(): lax.ppermute(held, 'heads', along(d))  9.89 us
    pallas_call x12, Pallas kernels, run(): pl.pallas_call(functools.partial(kernel, **static), out_shape=shapes, in_...  9.37 us
    all_to_all x1, starting transfers between devices, on_device(): later = lax.all_to_all(later, 'seq', 0, 0, axis_index_groups=backwards)  8.21 us
    all_to_all x1, waiting for transfers between devices, on_device(): before = lax.all_to_all(before, 'seq', 0, 0).reshape(width, DH)  7.89 us
    all_to_all x1, starting transfers between devices, on_device(): before = lax.all_to_all(before, 'seq', 0, 0).reshape(width, DH)  7.61 us
    ppermute x1, starting transfers between devices, on_device(): across = lax.ppermute(grad_out[None], 'heads', along(4))  6.97 us
  transfers between devices with their start and end apart: 8, of which 3 were waited for; matrix products, arithmetic and copies ran while one was open for 0% of the time, Pallas kernels for 7%

profile of v4, /device:TPU:8, one launch (start us, length us, event | category | flops | bytes accessed | tf_op | source)
XLA Modules:
  0.0 88.5 jit_solution(16795010480191765604)
XLA Ops:
  0.6 7.0 %collective-permute-start = (bf16[1,256,256]{2,1,0:T(8,128)(2,1)}, bf16[1,256,256]{2,1,0:T(8,128)(2,1)S(1)}, u32[]{:S(2)}, u32[]{:S(2)}) collective-permute-start(bf16[1,256,256]{2,1,0:T(8,128)(2,1)} %bitcast.8), channel_id=1, source_target_pairs={{0,256},{32,288},{64,320},{96,352},{128,384},{160,416},{192,448},{... | collective-permute-start | bytes 393224 | tf_op jit(solution)/shard_map/ppermute | solution.py:241
  7.6 2.1 %states.1 = f32[32,16,128]{2,1,0:T(8,128)} custom-call(bf16[256,256]{1,0:T(8,128)(2,1)} %k_ref.5, bf16[256,256]{1,0:T(8,128)(2,1)} %v_ref.5, bf16[128,256]{1,0:T(8,128)(2,1)} %sk_ref.1, bf16[128,256]{1,0:T(8,128)(2,1)} %sv_ref.1), custom_call_target="tpu_custom_call" | custom-call | flops 40000000000 | bytes 147600000 | tf_op jit(solution)/shard_map/states/pallas_call | solution.py:190
  9.7 13.2 %all-to-all-start = ((f32[32,16,128]{2,1,0:T(8,128)}), f32[32,16,128]{2,1,0:T(8,128)S(1)}, u32[]{:S(2)}, u32[]{:S(2)}) async-start(f32[32,16,128]{2,1,0:T(8,128)} %states.1), calls=%async_computation | async-start | bytes 524288 | tf_op jit(solution)/shard_map/all_to_all | solution.py:253
  23.0 0.1 pad_add_fusion.place_ref
  23.0 0.3 pack.1
  23.4 3.4 %collective-permute-start.3 = (bf16[2,256,256]{2,1,0:T(8,128)(2,1)S(1)}, bf16[2,256,256]{2,1,0:T(8,128)(2,1)S(1)}, u32[]{:S(2)}, u32[]{:S(2)}) collective-permute-start(bf16[2,256,256]{2,1,0:T(8,128)(2,1)S(1)} %pack.1), channel_id=1, source_target_pairs={{0,448},{32,96},{64,0},{96,160},{128,64},{160,224},{192,128},{224,... | collective-permute-start | bytes 786440 | tf_op jit(solution)/shard_map/ppermute | solution.py:252
  26.8 2.6 %collective-permute-start.2 = (bf16[2,256,256]{2,1,0:T(8,128)(2,1)S(1)}, bf16[2,256,256]{2,1,0:T(8,128)(2,1)S(1)}, u32[]{:S(2)}, u32[]{:S(2)}) collective-permute-start(bf16[2,256,256]{2,1,0:T(8,128)(2,1)S(1)} %pack.1), channel_id=1, source_target_pairs={{0,64},{32,480},{64,128},{96,32},{128,192},{160,96},{192,256},{224... | collective-permute-start | bytes 786440 | tf_op jit(solution)/shard_map/ppermute | solution.py:252
  29.4 3.9 %collective-permute-start.1 = (bf16[2,256,256]{2,1,0:T(8,128)(2,1)S(1)}, bf16[2,256,256]{2,1,0:T(8,128)(2,1)S(1)}, u32[]{:S(2)}, u32[]{:S(2)}) collective-permute-start(bf16[2,256,256]{2,1,0:T(8,128)(2,1)S(1)} %pack.1), channel_id=1, source_target_pairs={{0,128},{32,416},{64,192},{96,480},{128,256},{160,32},{192,320},{2... | collective-permute-start | bytes 786440 | tf_op jit(solution)/shard_map/ppermute | solution.py:252
  33.3 2.2 %all-to-all-done.in_ref = f32[32,16,128]{2,1,0:T(8,128)S(1)} async-done(((f32[32,16,128]{2,1,0:T(8,128)}), f32[32,16,128]{2,1,0:T(8,128)S(1)}, u32[]{:S(2)}, u32[]{:S(2)}) %all-to-all-start) | async-done | bytes 262176 | tf_op jit(solution)/shard_map/all_to_all | solution.py:253
  35.5 0.7 prefix.1._
  36.2 7.6 %all-to-all-start.1 = ((f32[32,8,128]{2,1,0:T(8,128)}), f32[32,8,128]{2,1,0:T(8,128)S(1)}, u32[]{:S(2)}, u32[]{:S(2)}) async-start(f32[32,8,128]{2,1,0:T(8,128)} %prefix.1._), calls=%async_computation.1 | async-start | bytes 262144 | tf_op jit(solution)/shard_map/all_to_all | solution.py:263
  43.9 0.5 within.1.within_ref.refs_0_
  44.4 0.1 pad_maximum_fusion.refs_0_
  44.6 1.9 %collective-permute-start.4 = (bf16[8,256,256]{2,1,0:T(8,128)(2,1)S(1)}, bf16[8,256,256]{2,1,0:T(8,128)(2,1)S(1)}, u32[]{:S(2)}, u32[]{:S(2)}) collective-permute-start(bf16[8,256,256]{2,1,0:T(8,128)(2,1)S(1)} %pad_maximum_fusion.refs_0_), channel_id=1, source_target_pairs={{0,32},{32,0},{64,96},{96,64},{128,160},{160,128},{192,224},{224,1... | collective-permute-start | bytes 3145736 | tf_op jit(solution)/shard_map/ppermute | solution.py:262
  46.5 7.9 %all-to-all-done.1 = f32[32,8,128]{2,1,0:T(8,128)S(1)} async-done(((f32[32,8,128]{2,1,0:T(8,128)}), f32[32,8,128]{2,1,0:T(8,128)S(1)}, u32[]{:S(2)}, u32[]{:S(2)}) %all-to-all-start.1) | async-done | bytes 131104 | tf_op jit(solution)/shard_map/all_to_all | solution.py:263
  54.4 0.2 forward.1.refs_4_.mix_ref
  54.6 1.4 %copy-done = bf16[256,4096]{1,0:T(8,128)(2,1)S(1)} copy-done((bf16[256,4096]{1,0:T(8,128)(2,1)S(1)}, bf16[256,4096]{1,0:T(8,128)(2,1)}, u32[]{:S(2)}) %copy-start) | copy-done | bytes 2097176
  56.0 1.7 %cotangent.1 = (f32[32,5,2,128]{3,2,1,0:T(2,128)S(1)}, bf16[256,256]{1,0:T(8,128)(2,1)S(1)}, bf16[256,256]{1,0:T(8,128)(2,1)S(1)}) custom-call(s32[2]{0:T(128)S(1)} %pad_add_fusion.place_ref, bf16[8,256,256]{2,1,0:T(8,128)(2,1)S(1)} %pad_maximum_fusion.refs_0_, bf16[8,256,256]{2,1,0:T(8,128)(2,1)S(1)} %collective-permute-done.4.refs_1_, ...), custom_call_target="tpu_custom_call" | custom-call | flops 3000000000 | bytes 11070000 | tf_op jit(solution)/shard_map/cotangent/pallas_call | solution.py:190
  57.7 13.6 %all_to_all.20.in_ref = f32[32,5,2,128]{3,2,1,0:T(2,128)S(1)} all-to-all(f32[32,5,2,128]{3,2,1,0:T(2,128)S(1)} %get-tuple-element.24), channel_id=1, replica_groups={{31,30,29,28,27,26,25,24,23,22,21,20,19,18,17,16,15,14,13,12,11,10,9,8,..., dimensions={0} | all-to-all | bytes 327680 | tf_op jit(solution)/shard_map/all_to_all | solution.py:276
  71.3 0.8 suffix.1
  72.1 8.2 %all-to-all-start.3 = ((f32[32,16,128]{2,1,0:T(8,128)}), f32[32,16,128]{2,1,0:T(8,128)S(1)}, u32[]{:S(2)}, u32[]{:S(2)}) async-start(f32[32,16,128]{2,1,0:T(8,128)} %get-tuple-element.25), calls=%async_computation.3 | async-start | bytes 524288 | tf_op jit(solution)/shard_map/all_to_all | solution.py:294
  80.3 1.9 %local.1 = (bf16[256,256]{1,0:T(8,128)(2,1)}, bf16[256,256]{1,0:T(8,128)(2,1)}, f32[256,256]{1,0:T(8,128)S(1)}, f32[256,256]{1,0:T(8,128)S(1)}) custom-call(bf16[256,256]{1,0:T(8,128)(2,1)S(1)} %copy-done.2, bf16[256,256]{1,0:T(8,128)(2,1)S(1)} %copy-done.3, bf16[256,256]{1,0:T(8,128)(2,1)S(1)} %copy-done.4, f32[256,128]{1,0:T(8,128)S(1)} %bitcast.7, ...), custom_call_target="tpu_custom_call" | custom-call | flops 3000000000 | bytes 11070000 | tf_op jit(solution)/shard_map/local/pallas_call | solution.py:190
  82.2 5.2 %all-to-all-done.3.s_ref = f32[32,16,128]{2,1,0:T(8,128)S(1)} async-done(((f32[32,16,128]{2,1,0:T(8,128)}), f32[32,16,128]{2,1,0:T(8,128)S(1)}, u32[]{:S(2)}, u32[]{:S(2)}) %all-to-all-start.3) | async-done | bytes 262176 | tf_op jit(solution)/shard_map/all_to_all | solution.py:294
  87.4 1.1 %final.1 = (bf16[256,256]{1,0:T(8,128)(2,1)}, bf16[256,256]{1,0:T(8,128)(2,1)}, bf16[128,256]{1,0:T(8,128)(2,1)}, bf16[128,256]{1,0:T(8,128)(2,1)}) custom-call(bf16[256,256]{1,0:T(8,128)(2,1)S(1)} %copy-done.3, bf16[256,256]{1,0:T(8,128)(2,1)S(1)} %copy-done.4, bf16[128,256]{1,0:T(8,128)(2,1)S(1)} %copy-done.5, bf16[128,256]{1,0:T(8,128)(2,1)S(1)} %copy-done.6, ...), custom_call_target="tpu_custom_call" | custom-call | flops 500000000 | bytes 1845000 | tf_op jit(solution)/shard_map/final/pallas_call | solution.py:190
  (23 shorter events, 0.1 us)
Async XLA Ops:
  0.6 22.4 %copy-start.1 = (bf16[256,256]{1,0:T(8,128)(2,1)S(1)}, bf16[256,256]{1,0:T(8,128)(2,1)}, u32[]{:S(2)}) copy-start(bf16[256,256]{1,0:T(8,128)(2,1)} %refs_2_.2) | copy-start | bytes 393220
  0.6 22.4 %collective-permute-start = (bf16[1,256,256]{2,1,0:T(8,128)(2,1)}, bf16[1,256,256]{2,1,0:T(8,128)(2,1)S(1)}, u32[]{:S(2)}, u32[]{:S(2)}) collective-permute-start(bf16[1,256,256]{2,1,0:T(8,128)(2,1)} %bitcast.8), channel_id=1, source_target_pairs={{0,256},{32,288},{64,320},{96,352},{128,384},{160,416},{192,448},{... | collective-permute-start | bytes 393224 | tf_op jit(solution)/shard_map/ppermute | solution.py:241
  9.7 25.8 %all-to-all-start = ((f32[32,16,128]{2,1,0:T(8,128)}), f32[32,16,128]{2,1,0:T(8,128)S(1)}, u32[]{:S(2)}, u32[]{:S(2)}) async-start(f32[32,16,128]{2,1,0:T(8,128)} %states.1), calls=%async_computation | async-start | bytes 524288 | tf_op jit(solution)/shard_map/all_to_all | solution.py:253
  23.4 20.5 %copy-start.2 = (bf16[256,256]{1,0:T(8,128)(2,1)S(1)}, bf16[256,256]{1,0:T(8,128)(2,1)}, u32[]{:S(2)}) copy-start(bf16[256,256]{1,0:T(8,128)(2,1)} %q_ref.5) | copy-start | bytes 393220
  23.4 20.5 %copy-start.3 = (bf16[256,256]{1,0:T(8,128)(2,1)S(1)}, bf16[256,256]{1,0:T(8,128)(2,1)}, u32[]{:S(2)}) copy-start(bf16[256,256]{1,0:T(8,128)(2,1)} %k_ref.5) | copy-start | bytes 393220
  23.4 20.5 %copy-start.4 = (bf16[256,256]{1,0:T(8,128)(2,1)S(1)}, bf16[256,256]{1,0:T(8,128)(2,1)}, u32[]{:S(2)}) copy-start(bf16[256,256]{1,0:T(8,128)(2,1)} %v_ref.5) | copy-start | bytes 393220
  23.4 20.9 %collective-permute-start.3 = (bf16[2,256,256]{2,1,0:T(8,128)(2,1)S(1)}, bf16[2,256,256]{2,1,0:T(8,128)(2,1)S(1)}, u32[]{:S(2)}, u32[]{:S(2)}) collective-permute-start(bf16[2,256,256]{2,1,0:T(8,128)(2,1)S(1)} %pack.1), channel_id=1, source_target_pairs={{0,448},{32,96},{64,0},{96,160},{128,64},{160,224},{192,128},{224,... | collective-permute-start | bytes 786440 | tf_op jit(solution)/shard_map/ppermute | solution.py:252
  26.8 17.6 %collective-permute-start.2 = (bf16[2,256,256]{2,1,0:T(8,128)(2,1)S(1)}, bf16[2,256,256]{2,1,0:T(8,128)(2,1)S(1)}, u32[]{:S(2)}, u32[]{:S(2)}) collective-permute-start(bf16[2,256,256]{2,1,0:T(8,128)(2,1)S(1)} %pack.1), channel_id=1, source_target_pairs={{0,64},{32,480},{64,128},{96,32},{128,192},{160,96},{192,256},{224... | collective-permute-start | bytes 786440 | tf_op jit(solution)/shard_map/ppermute | solution.py:252
  29.4 15.0 %collective-permute-start.1 = (bf16[2,256,256]{2,1,0:T(8,128)(2,1)S(1)}, bf16[2,256,256]{2,1,0:T(8,128)(2,1)S(1)}, u32[]{:S(2)}, u32[]{:S(2)}) collective-permute-start(bf16[2,256,256]{2,1,0:T(8,128)(2,1)S(1)} %pack.1), channel_id=1, source_target_pairs={{0,128},{32,416},{64,192},{96,480},{128,256},{160,32},{192,320},{2... | collective-permute-start | bytes 786440 | tf_op jit(solution)/shard_map/ppermute | solution.py:252
  36.2 18.2 %all-to-all-start.1 = ((f32[32,8,128]{2,1,0:T(8,128)}), f32[32,8,128]{2,1,0:T(8,128)S(1)}, u32[]{:S(2)}, u32[]{:S(2)}) async-start(f32[32,8,128]{2,1,0:T(8,128)} %prefix.1._), calls=%async_computation.1 | async-start | bytes 262144 | tf_op jit(solution)/shard_map/all_to_all | solution.py:263
  44.6 10.0 %collective-permute-start.4 = (bf16[8,256,256]{2,1,0:T(8,128)(2,1)S(1)}, bf16[8,256,256]{2,1,0:T(8,128)(2,1)S(1)}, u32[]{:S(2)}, u32[]{:S(2)}) collective-permute-start(bf16[8,256,256]{2,1,0:T(8,128)(2,1)S(1)} %pad_maximum_fusion.refs_0_), channel_id=1, source_target_pairs={{0,32},{32,0},{64,96},{96,64},{128,160},{160,128},{192,224},{224,1... | collective-permute-start | bytes 3145736 | tf_op jit(solution)/shard_map/ppermute | solution.py:262
  54.4 1.6 %copy-start = (bf16[256,4096]{1,0:T(8,128)(2,1)S(1)}, bf16[256,4096]{1,0:T(8,128)(2,1)}, u32[]{:S(2)}) copy-start(bf16[256,4096]{1,0:T(8,128)(2,1)} %refs_2_.3) | copy-start | bytes 6291460
  54.4 1.6 %copy-start.7 = (f32[256]{0:T(256)S(1)}, f32[256]{0:T(256)}, u32[]{:S(2)}) copy-start(f32[256]{0:T(256)} %param.13) | copy-start | bytes 3076
  72.1 15.3 %all-to-all-start.3 = ((f32[32,16,128]{2,1,0:T(8,128)}), f32[32,16,128]{2,1,0:T(8,128)S(1)}, u32[]{:S(2)}, u32[]{:S(2)}) async-start(f32[32,16,128]{2,1,0:T(8,128)} %get-tuple-element.25), calls=%async_computation.3 | async-start | bytes 524288 | tf_op jit(solution)/shard_map/all_to_all | solution.py:294
  80.3 7.1 %copy-start.5 = (bf16[128,256]{1,0:T(8,128)(2,1)S(1)}, bf16[128,256]{1,0:T(8,128)(2,1)}, u32[]{:S(2)}) copy-start(bf16[128,256]{1,0:T(8,128)(2,1)} %sk_ref.1) | copy-start | bytes 196612
  80.3 7.1 %copy-start.6 = (bf16[128,256]{1,0:T(8,128)(2,1)S(1)}, bf16[128,256]{1,0:T(8,128)(2,1)}, u32[]{:S(2)}) copy-start(bf16[128,256]{1,0:T(8,128)(2,1)} %sv_ref.1) | copy-start | bytes 196612

commit v5 on v4

--- a/solution.py
+++ b/solution.py
@@ -21,6 +21,10 @@
 def halves(x):
     high = x.astype(bf16)
     return high, (x - high.astype(f32)).astype(bf16)
+
+
+def beside(a, b):
+    return jnp.concatenate([a, b], axis=1)
 
 
 def head(h):
@@ -84,7 +88,7 @@
     for h in range(heads):
         q = q_ref[:, head(h)]
         c_high, c_low = halves(c_ref[head(h), :])
-        mixture = within_ref[:, head(h)] + dot(q, c_high, 1, 0) + dot(q, c_low, 1, 0)
+        mixture = within_ref[:, head(h)] + dot(beside(q, q), jnp.concatenate([c_high, c_low], axis=0), 1, 0)
         mix_ref[:, head(h)] = mixture
 
 
@@ -116,7 +120,8 @@
         high_ref[:, head(h)] = high
         low_ref[:, head(h)] = low
         q = q_ref[:, head(h)]
-        outer = dot(q, high, 0, 0) + dot(q, low, 0, 0)
+        outer = dot(q, beside(high, low), 0, 0)
+        outer = outer[:, :DH] + outer[:, DH:]
         for at in range(0, DH, heads):
             out_ref[h * per + at // rows, at % rows // heads] = outer[at : at + heads, :]
     gain = jnp.concatenate(gains, axis=0)
@@ -168,10 +173,10 @@
         l_high, l_low = halves(later)
         t_high, t_low = halves(total)
         k, v, sk, sv = k_ref[:, head(h)], v_ref[:, head(h)], sk_ref[:, head(h)], sv_ref[:, head(h)]
-        out_k[:, head(h)] = (gk_ref[:, head(h)] + dot(v, l_high, 1, 1) + dot(v, l_low, 1, 1)).astype(bf16)
-        out_v[:, head(h)] = (gv_ref[:, head(h)] + dot(k, l_high, 1, 0) + dot(k, l_low, 1, 0)).astype(bf16)
-        out_sk[:, head(h)] = (dot(sv, t_high, 1, 1) + dot(sv, t_low, 1, 1)).astype(bf16)
-        out_sv[:, head(h)] = (dot(sk, t_high, 1, 0) + dot(sk, t_low, 1, 0)).astype(bf16)
+        out_k[:, head(h)] = (gk_ref[:, head(h)] + dot(beside(v, v), beside(l_high, l_low), 1, 1)).astype(bf16)
+        out_v[:, head(h)] = (gv_ref[:, head(h)] + dot(beside(k, k), jnp.concatenate([l_high, l_low], axis=0), 1, 0)).astype(bf16)
+        out_sk[:, head(h)] = (dot(beside(sv, sv), beside(t_high, t_low), 1, 1)).astype(bf16)
+        out_sv[:, head(h)] = (dot(beside(sk, sk), jnp.concatenate([t_high, t_low], axis=0), 1, 0)).astype(bf16)
 
 
 WHOLE = pl.BlockSpec(memory_space=pltpu.VMEM)

time: 89 us -> 89 us (level)
  no operation moved by 1% of the time
where the time goes in v5:
time: 89 us; the launch traced here: 88.4 us
  starting transfers between devices  47.8 us (54%)
  waiting for transfers between devices  15.3 us (17%)
  blocking collectives  13.6 us (15%)
  Pallas kernels  9.3 us (10%)
  local copies, waits for them, and re-layouts  1.4 us (2%)
  between operations  0.89 us (1%)
    all_to_all x1, blocking collectives, on_device(): outer = lax.all_to_all(outer, 'seq', 0, 0, axis_index_groups=backwards)  13.6 us
    all_to_all x1, starting transfers between devices, on_device(): own = lax.all_to_all(own, 'seq', 0, 0)  13.2 us
    ppermute x3, starting transfers between devices, on_device(): lax.ppermute(held, 'heads', along(d))  9.89 us
    pallas_call x12, Pallas kernels, run(): pl.pallas_call(functools.partial(kernel, **static), out_shape=shapes, in_...  9.3 us
    all_to_all x1, starting transfers between devices, on_device(): later = lax.all_to_all(later, 'seq', 0, 0, axis_index_groups=backwards)  8.21 us
    all_to_all x1, waiting for transfers between devices, on_device(): before = lax.all_to_all(before, 'seq', 0, 0).reshape(width, DH)  7.89 us
    all_to_all x1, starting transfers between devices, on_device(): before = lax.all_to_all(before, 'seq', 0, 0).reshape(width, DH)  7.61 us
    ppermute x1, starting transfers between devices, on_device(): across = lax.ppermute(grad_out[None], 'heads', along(4))  6.97 us
  transfers between devices with their start and end apart: 8, of which 3 were waited for; matrix products, arithmetic and copies ran while one was open for 0% of the time, Pallas kernels for 7%

profile of v5, /device:TPU:8, one launch (start us, length us, event | category | flops | bytes accessed | tf_op | source)
XLA Modules:
  0.0 88.4 jit_solution(17721078117720840190)
XLA Ops:
  0.6 7.0 %collective-permute-start = (bf16[1,256,256]{2,1,0:T(8,128)(2,1)}, bf16[1,256,256]{2,1,0:T(8,128)(2,1)S(1)}, u32[]{:S(2)}, u32[]{:S(2)}) collective-permute-start(bf16[1,256,256]{2,1,0:T(8,128)(2,1)} %bitcast.8), channel_id=1, source_target_pairs={{0,256},{32,288},{64,320},{96,352},{128,384},{160,416},{192,448},{... | collective-permute-start | bytes 393224 | tf_op jit(solution)/shard_map/ppermute | solution.py:246
  7.6 2.1 %states.1 = f32[32,16,128]{2,1,0:T(8,128)} custom-call(bf16[256,256]{1,0:T(8,128)(2,1)} %k_ref.5, bf16[256,256]{1,0:T(8,128)(2,1)} %v_ref.5, bf16[128,256]{1,0:T(8,128)(2,1)} %sk_ref.1, bf16[128,256]{1,0:T(8,128)(2,1)} %sv_ref.1), custom_call_target="tpu_custom_call" | custom-call | flops 40000000000 | bytes 147600000 | tf_op jit(solution)/shard_map/states/pallas_call | solution.py:195
  9.7 13.2 %all-to-all-start = ((f32[32,16,128]{2,1,0:T(8,128)}), f32[32,16,128]{2,1,0:T(8,128)S(1)}, u32[]{:S(2)}, u32[]{:S(2)}) async-start(f32[32,16,128]{2,1,0:T(8,128)} %states.1), calls=%async_computation | async-start | bytes 524288 | tf_op jit(solution)/shard_map/all_to_all | solution.py:258
  23.0 0.1 pad_add_fusion.place_ref
  23.0 0.3 pack.1
  23.4 3.4 %collective-permute-start.3 = (bf16[2,256,256]{2,1,0:T(8,128)(2,1)S(1)}, bf16[2,256,256]{2,1,0:T(8,128)(2,1)S(1)}, u32[]{:S(2)}, u32[]{:S(2)}) collective-permute-start(bf16[2,256,256]{2,1,0:T(8,128)(2,1)S(1)} %pack.1), channel_id=1, source_target_pairs={{0,448},{32,96},{64,0},{96,160},{128,64},{160,224},{192,128},{224,... | collective-permute-start | bytes 786440 | tf_op jit(solution)/shard_map/ppermute | solution.py:257
  26.8 2.6 %collective-permute-start.2 = (bf16[2,256,256]{2,1,0:T(8,128)(2,1)S(1)}, bf16[2,256,256]{2,1,0:T(8,128)(2,1)S(1)}, u32[]{:S(2)}, u32[]{:S(2)}) collective-permute-start(bf16[2,256,256]{2,1,0:T(8,128)(2,1)S(1)} %pack.1), channel_id=1, source_target_pairs={{0,64},{32,480},{64,128},{96,32},{128,192},{160,96},{192,256},{224... | collective-permute-start | bytes 786440 | tf_op jit(solution)/shard_map/ppermute | solution.py:257
  29.4 3.9 %collective-permute-start.1 = (bf16[2,256,256]{2,1,0:T(8,128)(2,1)S(1)}, bf16[2,256,256]{2,1,0:T(8,128)(2,1)S(1)}, u32[]{:S(2)}, u32[]{:S(2)}) collective-permute-start(bf16[2,256,256]{2,1,0:T(8,128)(2,1)S(1)} %pack.1), channel_id=1, source_target_pairs={{0,128},{32,416},{64,192},{96,480},{128,256},{160,32},{192,320},{2... | collective-permute-start | bytes 786440 | tf_op jit(solution)/shard_map/ppermute | solution.py:257
  33.3 2.2 %all-to-all-done.in_ref = f32[32,16,128]{2,1,0:T(8,128)S(1)} async-done(((f32[32,16,128]{2,1,0:T(8,128)}), f32[32,16,128]{2,1,0:T(8,128)S(1)}, u32[]{:S(2)}, u32[]{:S(2)}) %all-to-all-start) | async-done | bytes 262176 | tf_op jit(solution)/shard_map/all_to_all | solution.py:258
  35.5 0.7 prefix.1._
  36.2 7.6 %all-to-all-start.1 = ((f32[32,8,128]{2,1,0:T(8,128)}), f32[32,8,128]{2,1,0:T(8,128)S(1)}, u32[]{:S(2)}, u32[]{:S(2)}) async-start(f32[32,8,128]{2,1,0:T(8,128)} %prefix.1._), calls=%async_computation.1 | async-start | bytes 262144 | tf_op jit(solution)/shard_map/all_to_all | solution.py:268
  43.9 0.5 within.1.within_ref.refs_0_
  44.4 0.1 pad_maximum_fusion.refs_0_
  44.6 1.9 %collective-permute-start.4 = (bf16[8,256,256]{2,1,0:T(8,128)(2,1)S(1)}, bf16[8,256,256]{2,1,0:T(8,128)(2,1)S(1)}, u32[]{:S(2)}, u32[]{:S(2)}) collective-permute-start(bf16[8,256,256]{2,1,0:T(8,128)(2,1)S(1)} %pad_maximum_fusion.refs_0_), channel_id=1, source_target_pairs={{0,32},{32,0},{64,96},{96,64},{128,160},{160,128},{192,224},{224,1... | collective-permute-start | bytes 3145736 | tf_op jit(solution)/shard_map/ppermute | solution.py:267
  46.5 7.9 %all-to-all-done.1 = f32[32,8,128]{2,1,0:T(8,128)S(1)} async-done(((f32[32,8,128]{2,1,0:T(8,128)}), f32[32,8,128]{2,1,0:T(8,128)S(1)}, u32[]{:S(2)}, u32[]{:S(2)}) %all-to-all-start.1) | async-done | bytes 131104 | tf_op jit(solution)/shard_map/all_to_all | solution.py:268
  54.4 0.2 forward.1.refs_4_.mix_ref
  54.6 1.4 %copy-done = bf16[256,4096]{1,0:T(8,128)(2,1)S(1)} copy-done((bf16[256,4096]{1,0:T(8,128)(2,1)S(1)}, bf16[256,4096]{1,0:T(8,128)(2,1)}, u32[]{:S(2)}) %copy-start) | copy-done | bytes 2097176
  56.0 1.7 %cotangent.1 = (f32[32,5,2,128]{3,2,1,0:T(2,128)S(1)}, bf16[256,256]{1,0:T(8,128)(2,1)S(1)}, bf16[256,256]{1,0:T(8,128)(2,1)S(1)}) custom-call(s32[2]{0:T(128)S(1)} %pad_add_fusion.place_ref, bf16[8,256,256]{2,1,0:T(8,128)(2,1)S(1)} %pad_maximum_fusion.refs_0_, bf16[8,256,256]{2,1,0:T(8,128)(2,1)S(1)} %collective-permute-done.4.refs_1_, ...), custom_call_target="tpu_custom_call" | custom-call | flops 3000000000 | bytes 11070000 | tf_op jit(solution)/shard_map/cotangent/pallas_call | solution.py:195
  57.7 13.6 %all_to_all.20.in_ref = f32[32,5,2,128]{3,2,1,0:T(2,128)S(1)} all-to-all(f32[32,5,2,128]{3,2,1,0:T(2,128)S(1)} %get-tuple-element.24), channel_id=1, replica_groups={{31,30,29,28,27,26,25,24,23,22,21,20,19,18,17,16,15,14,13,12,11,10,9,8,..., dimensions={0} | all-to-all | bytes 327680 | tf_op jit(solution)/shard_map/all_to_all | solution.py:281
  71.3 0.8 suffix.1
  72.0 8.2 %all-to-all-start.3 = ((f32[32,16,128]{2,1,0:T(8,128)}), f32[32,16,128]{2,1,0:T(8,128)S(1)}, u32[]{:S(2)}, u32[]{:S(2)}) async-start(f32[32,16,128]{2,1,0:T(8,128)} %get-tuple-element.25), calls=%async_computation.3 | async-start | bytes 524288 | tf_op jit(solution)/shard_map/all_to_all | solution.py:299
  80.3 1.9 %local.1 = (bf16[256,256]{1,0:T(8,128)(2,1)}, bf16[256,256]{1,0:T(8,128)(2,1)}, f32[256,256]{1,0:T(8,128)S(1)}, f32[256,256]{1,0:T(8,128)S(1)}) custom-call(bf16[256,256]{1,0:T(8,128)(2,1)S(1)} %copy-done.2, bf16[256,256]{1,0:T(8,128)(2,1)S(1)} %copy-done.3, bf16[256,256]{1,0:T(8,128)(2,1)S(1)} %copy-done.4, f32[256,128]{1,0:T(8,128)S(1)} %bitcast.7, ...), custom_call_target="tpu_custom_call" | custom-call | flops 3000000000 | bytes 11070000 | tf_op jit(solution)/shard_map/local/pallas_call | solution.py:195
  82.2 5.2 %all-to-all-done.3.s_ref = f32[32,16,128]{2,1,0:T(8,128)S(1)} async-done(((f32[32,16,128]{2,1,0:T(8,128)}), f32[32,16,128]{2,1,0:T(8,128)S(1)}, u32[]{:S(2)}, u32[]{:S(2)}) %all-to-all-start.3) | async-done | bytes 262176 | tf_op jit(solution)/shard_map/all_to_all | solution.py:299
  87.4 1.1 %final.1 = (bf16[256,256]{1,0:T(8,128)(2,1)}, bf16[256,256]{1,0:T(8,128)(2,1)}, bf16[128,256]{1,0:T(8,128)(2,1)}, bf16[128,256]{1,0:T(8,128)(2,1)}) custom-call(bf16[256,256]{1,0:T(8,128)(2,1)S(1)} %copy-done.3, bf16[256,256]{1,0:T(8,128)(2,1)S(1)} %copy-done.4, bf16[128,256]{1,0:T(8,128)(2,1)S(1)} %copy-done.5, bf16[128,256]{1,0:T(8,128)(2,1)S(1)} %copy-done.6, ...), custom_call_target="tpu_custom_call" | custom-call | flops 500000000 | bytes 1845000 | tf_op jit(solution)/shard_map/final/pallas_call | solution.py:195
  (23 shorter events, 0.1 us)
Async XLA Ops:
  0.6 22.4 %copy-start.1 = (bf16[256,256]{1,0:T(8,128)(2,1)S(1)}, bf16[256,256]{1,0:T(8,128)(2,1)}, u32[]{:S(2)}) copy-start(bf16[256,256]{1,0:T(8,128)(2,1)} %refs_2_.2) | copy-start | bytes 393220
  0.6 22.4 %collective-permute-start = (bf16[1,256,256]{2,1,0:T(8,128)(2,1)}, bf16[1,256,256]{2,1,0:T(8,128)(2,1)S(1)}, u32[]{:S(2)}, u32[]{:S(2)}) collective-permute-start(bf16[1,256,256]{2,1,0:T(8,128)(2,1)} %bitcast.8), channel_id=1, source_target_pairs={{0,256},{32,288},{64,320},{96,352},{128,384},{160,416},{192,448},{... | collective-permute-start | bytes 393224 | tf_op jit(solution)/shard_map/ppermute | solution.py:246
  9.7 25.8 %all-to-all-start = ((f32[32,16,128]{2,1,0:T(8,128)}), f32[32,16,128]{2,1,0:T(8,128)S(1)}, u32[]{:S(2)}, u32[]{:S(2)}) async-start(f32[32,16,128]{2,1,0:T(8,128)} %states.1), calls=%async_computation | async-start | bytes 524288 | tf_op jit(solution)/shard_map/all_to_all | solution.py:258
  23.4 20.5 %copy-start.2 = (bf16[256,256]{1,0:T(8,128)(2,1)S(1)}, bf16[256,256]{1,0:T(8,128)(2,1)}, u32[]{:S(2)}) copy-start(bf16[256,256]{1,0:T(8,128)(2,1)} %q_ref.5) | copy-start | bytes 393220
  23.4 20.5 %copy-start.3 = (bf16[256,256]{1,0:T(8,128)(2,1)S(1)}, bf16[256,256]{1,0:T(8,128)(2,1)}, u32[]{:S(2)}) copy-start(bf16[256,256]{1,0:T(8,128)(2,1)} %k_ref.5) | copy-start | bytes 393220
  23.4 20.5 %copy-start.4 = (bf16[256,256]{1,0:T(8,128)(2,1)S(1)}, bf16[256,256]{1,0:T(8,128)(2,1)}, u32[]{:S(2)}) copy-start(bf16[256,256]{1,0:T(8,128)(2,1)} %v_ref.5) | copy-start | bytes 393220
  23.4 20.9 %collective-permute-start.3 = (bf16[2,256,256]{2,1,0:T(8,128)(2,1)S(1)}, bf16[2,256,256]{2,1,0:T(8,128)(2,1)S(1)}, u32[]{:S(2)}, u32[]{:S(2)}) collective-permute-start(bf16[2,256,256]{2,1,0:T(8,128)(2,1)S(1)} %pack.1), channel_id=1, source_target_pairs={{0,448},{32,96},{64,0},{96,160},{128,64},{160,224},{192,128},{224,... | collective-permute-start | bytes 786440 | tf_op jit(solution)/shard_map/ppermute | solution.py:257
  26.8 17.6 %collective-permute-start.2 = (bf16[2,256,256]{2,1,0:T(8,128)(2,1)S(1)}, bf16[2,256,256]{2,1,0:T(8,128)(2,1)S(1)}, u32[]{:S(2)}, u32[]{:S(2)}) collective-permute-start(bf16[2,256,256]{2,1,0:T(8,128)(2,1)S(1)} %pack.1), channel_id=1, source_target_pairs={{0,64},{32,480},{64,128},{96,32},{128,192},{160,96},{192,256},{224... | collective-permute-start | bytes 786440 | tf_op jit(solution)/shard_map/ppermute | solution.py:257
  29.4 15.0 %collective-permute-start.1 = (bf16[2,256,256]{2,1,0:T(8,128)(2,1)S(1)}, bf16[2,256,256]{2,1,0:T(8,128)(2,1)S(1)}, u32[]{:S(2)}, u32[]{:S(2)}) collective-permute-start(bf16[2,256,256]{2,1,0:T(8,128)(2,1)S(1)} %pack.1), channel_id=1, source_target_pairs={{0,128},{32,416},{64,192},{96,480},{128,256},{160,32},{192,320},{2... | collective-permute-start | bytes 786440 | tf_op jit(solution)/shard_map/ppermute | solution.py:257
  36.2 18.2 %all-to-all-start.1 = ((f32[32,8,128]{2,1,0:T(8,128)}), f32[32,8,128]{2,1,0:T(8,128)S(1)}, u32[]{:S(2)}, u32[]{:S(2)}) async-start(f32[32,8,128]{2,1,0:T(8,128)} %prefix.1._), calls=%async_computation.1 | async-start | bytes 262144 | tf_op jit(solution)/shard_map/all_to_all | solution.py:268
  44.6 10.0 %collective-permute-start.4 = (bf16[8,256,256]{2,1,0:T(8,128)(2,1)S(1)}, bf16[8,256,256]{2,1,0:T(8,128)(2,1)S(1)}, u32[]{:S(2)}, u32[]{:S(2)}) collective-permute-start(bf16[8,256,256]{2,1,0:T(8,128)(2,1)S(1)} %pad_maximum_fusion.refs_0_), channel_id=1, source_target_pairs={{0,32},{32,0},{64,96},{96,64},{128,160},{160,128},{192,224},{224,1... | collective-permute-start | bytes 3145736 | tf_op jit(solution)/shard_map/ppermute | solution.py:267
  54.4 1.6 %copy-start = (bf16[256,4096]{1,0:T(8,128)(2,1)S(1)}, bf16[256,4096]{1,0:T(8,128)(2,1)}, u32[]{:S(2)}) copy-start(bf16[256,4096]{1,0:T(8,128)(2,1)} %refs_2_.3) | copy-start | bytes 6291460
  54.4 1.6 %copy-start.7 = (f32[256]{0:T(256)S(1)}, f32[256]{0:T(256)}, u32[]{:S(2)}) copy-start(f32[256]{0:T(256)} %param.13) | copy-start | bytes 3076
  72.0 15.3 %all-to-all-start.3 = ((f32[32,16,128]{2,1,0:T(8,128)}), f32[32,16,128]{2,1,0:T(8,128)S(1)}, u32[]{:S(2)}, u32[]{:S(2)}) async-start(f32[32,16,128]{2,1,0:T(8,128)} %get-tuple-element.25), calls=%async_computation.3 | async-start | bytes 524288 | tf_op jit(solution)/shard_map/all_to_all | solution.py:299
  80.3 7.1 %copy-start.5 = (bf16[128,256]{1,0:T(8,128)(2,1)S(1)}, bf16[128,256]{1,0:T(8,128)(2,1)}, u32[]{:S(2)}) copy-start(bf16[128,256]{1,0:T(8,128)(2,1)} %sk_ref.1) | copy-start | bytes 196612
  80.3 7.1 %copy-start.6 = (bf16[128,256]{1,0:T(8,128)(2,1)S(1)}, bf16[128,256]{1,0:T(8,128)(2,1)}, u32[]{:S(2)}) copy-start(bf16[128,256]{1,0:T(8,128)(2,1)} %sv_ref.1) | copy-start | bytes 196612

commit v6 on v5

--- a/solution.py
+++ b/solution.py
@@ -84,17 +84,27 @@
         out_ref[:, head(h)] = dot(high, v, 1, 0) + dot(low, v, 1, 0)
 
 
-def forward_kernel(q_ref, within_ref, c_ref, mix_ref, *, heads):
-    for h in range(heads):
-        q = q_ref[:, head(h)]
-        c_high, c_low = halves(c_ref[head(h), :])
-        mixture = within_ref[:, head(h)] + dot(beside(q, q), jnp.concatenate([c_high, c_low], axis=0), 1, 0)
-        mix_ref[:, head(h)] = mixture
+def narrow_kernel(c_ref, high_ref, low_ref):
+    high_ref[...], low_ref[...] = halves(c_ref[...])
 
 
 def cotangent_kernel(place_ref, *refs, heads, rows, parts):
     held = refs[: len(parts)]
-    w_ref, q_ref, mix_ref, gain_ref, out_ref, high_ref, low_ref = refs[len(parts) :]
+    w_hbm, gain_hbm, q_ref, within_ref, ch_ref, cl_ref, out_ref, high_ref, low_ref, mix_ref, w_ref, gain_ref, sems = refs[len(parts) :]
+    pieces = sems.shape[0] - 1
+    height = w_ref.shape[0] // pieces
+    loads = [pltpu.make_async_copy(gain_hbm, gain_ref, sems.at[pieces])]
+    for i in range(pieces):
+        piece = slice(i * height, (i + 1) * height)
+        loads.append(pltpu.make_async_copy(w_hbm.at[piece], w_ref.at[piece], sems.at[i]))
+    for load in loads:
+        load.start()
+    for h in range(heads):
+        q = q_ref[:, head(h)]
+        both = jnp.concatenate([ch_ref[head(h), :], cl_ref[head(h), :]], axis=0)
+        mix_ref[:, head(h)] = within_ref[:, head(h)] + dot(beside(q, q), both, 1, 0)
+    for load in loads:
+        load.wait()
     length, width = held[0].shape[1:]
     chip, core = place_ref[0], place_ref[1]
     chips = w_ref.shape[1] // (2 * width)
@@ -129,7 +139,7 @@
 
 
 def local_kernel(
-    q_ref, k_ref, v_ref, c_ref, mix_ref, gain_ref, gh_ref, gl_ref, att_ref, gq_ref, gk_ref, gv_ref, *, heads, self_scale
+    q_ref, k_ref, v_ref, ch_ref, cl_ref, mix_ref, gain_ref, gh_ref, gl_ref, att_ref, gq_ref, gk_ref, gv_ref, *, heads, self_scale
 ):
     for h in range(heads):
         mixture = mix_ref[:, head(h)]
@@ -140,7 +150,7 @@
         causal, (m_high, m_low) = masked_scores(q, k, self_scale)
         scores = jnp.where(causal, dot(high, v, 1, 1) + dot(low, v, 1, 1), 0.0) * self_scale
         s_high, s_low = halves(scores)
-        c_high, c_low = halves(c_ref[head(h), :])
+        c_high, c_low = ch_ref[head(h), :], cl_ref[head(h), :]
         grad_query = dot(s_high, k, 1, 0) + dot(s_low, k, 1, 0)
         grad_query = grad_query + dot(high, c_high, 1, 1) + dot(high, c_low, 1, 1) + dot(low, c_high, 1, 1)
         gq_ref[:, head(h)] = grad_query.astype(bf16)
@@ -165,18 +175,35 @@
             out_ref[j, rows + at : rows + at + heads, :] = total
 
 
-def final_kernel(k_ref, v_ref, sk_ref, sv_ref, s_ref, gk_ref, gv_ref, out_k, out_v, out_sk, out_sv, *, heads, rows):
+def final_kernel(
+    k_ref, v_ref, sk_ref, sv_ref, s_ref, gk_ref, gv_ref, k_hbm, v_hbm, sk_hbm, sv_hbm, out_k, out_v, out_sk, out_sv, sems, *, heads, rows
+):
     per = DH // rows
+    pairs = ((out_k, k_hbm), (out_v, v_hbm), (out_sk, sk_hbm), (out_sv, sv_hbm))
+    stores = [pltpu.make_async_copy(a, b, sems.at[i]) for i, (a, b) in enumerate(pairs)]
+    both = []
     for h in range(heads):
         later = s_ref[h * per : (h + 1) * per, :rows, :].reshape(DH, DH)
         total = s_ref[h * per : (h + 1) * per, rows:, :].reshape(DH, DH)
-        l_high, l_low = halves(later)
-        t_high, t_low = halves(total)
-        k, v, sk, sv = k_ref[:, head(h)], v_ref[:, head(h)], sk_ref[:, head(h)], sv_ref[:, head(h)]
-        out_k[:, head(h)] = (gk_ref[:, head(h)] + dot(beside(v, v), beside(l_high, l_low), 1, 1)).astype(bf16)
-        out_v[:, head(h)] = (gv_ref[:, head(h)] + dot(beside(k, k), jnp.concatenate([l_high, l_low], axis=0), 1, 0)).astype(bf16)
-        out_sk[:, head(h)] = (dot(beside(sv, sv), beside(t_high, t_low), 1, 1)).astype(bf16)
-        out_sv[:, head(h)] = (dot(beside(sk, sk), jnp.concatenate([t_high, t_low], axis=0), 1, 0)).astype(bf16)
+        both.append((head(h), *halves(later), *halves(total)))
+    for at, l_high, l_low, _, _ in both:
+        v = v_ref[:, at]
+        out_k[:, at] = (gk_ref[:, at] + dot(beside(v, v), beside(l_high, l_low), 1, 1)).astype(bf16)
+    stores[0].start()
+    for at, l_high, l_low, _, _ in both:
+        k = k_ref[:, at]
+        out_v[:, at] = (gv_ref[:, at] + dot(beside(k, k), jnp.concatenate([l_high, l_low], axis=0), 1, 0)).astype(bf16)
+    stores[1].start()
+    for at, _, _, t_high, t_low in both:
+        sv = sv_ref[:, at]
+        out_sk[:, at] = (dot(beside(sv, sv), beside(t_high, t_low), 1, 1)).astype(bf16)
+    stores[2].start()
+    for at, _, _, t_high, t_low in both:
+        sk = sk_ref[:, at]
+        out_sv[:, at] = (dot(beside(sk, sk), jnp.concatenate([t_high, t_low], axis=0), 1, 0)).astype(bf16)
+    stores[3].start()
+    for store in stores:
+        store.wait()
 
 
 WHOLE = pl.BlockSpec(memory_space=pltpu.VMEM)
@@ -185,7 +212,7 @@
 HBM = pl.BlockSpec(memory_space=pltpu.HBM)
 
 
-MICROSECONDS = {"states": 40, "pack": 40, "within": 40, "forward": 40, "cotangent": 3, "local": 3}
+MICROSECONDS = {"states": 40, "pack": 40, "within": 40, "narrow": 40, "cotangent": 3, "local": 3}
 
 
 def call(kernel, outs, name, ins=None, scratch=(), aliases=None, out_specs=None, **static):
@@ -266,18 +293,19 @@
     whole = jnp.concatenate([held, second, above, below], axis=0)
     other = lax.ppermute(whole, "heads", [(i, i ^ 1) for i in range(groups)])
     before = lax.all_to_all(before, "seq", 0, 0).reshape(width, DH)
-    (mixture,) = call(forward_kernel, [((length, width), f32)], "forward", heads=heads)(queries, within, before)
+    narrow = call(narrow_kernel, [((width, DH), bf16)] * 2, "narrow")(before)
     blocks = [whole, other]
     parts = [[(d, swapped, None) for d in steps] for swapped in (False, True) for steps in ((0, 4, 2, 6, 1, 5, 7, 3),)]
-    outer, g_high, g_low = call(
+    outer, g_high, g_low, mixture = call(
         cotangent_kernel,
-        [((count, rows // heads + 1, heads, DH), f32), ((length, width), bf16), ((length, width), bf16)],
+        [((count, rows // heads + 1, heads, DH), f32), ((length, width), bf16), ((length, width), bf16), ((length, width), f32)],
         "cotangent",
-        ins=[SCALAR] + [WHOLE] * (len(blocks) + 4),
+        ins=[SCALAR] + [WHOLE] * len(blocks) + [HBM, HBM] + [WHOLE] * 4,
+        scratch=[pltpu.VMEM(x.shape, x.dtype) for x in (out_weight, gain)] + [pltpu.SemaphoreType.DMA((9,))],
         heads=heads,
         rows=rows,
         parts=parts,
-    )(place, *blocks, out_weight, queries, mixture, gain)
+    )(place, *blocks, *(pltpu.with_memory_space_constraint(x, pltpu.HBM) for x in (out_weight, gain)), queries, within, *narrow)
     outer = lax.all_to_all(outer, "seq", 0, 0, axis_index_groups=backwards)
     attended, grad_query, grad_key, grad_value = call(
         local_kernel,
@@ -285,7 +313,7 @@
         "local",
         heads=heads,
         self_scale=self_scale,
-    )(queries, keys, values, before, mixture, gain, g_high, g_low)
+    )(queries, keys, values, *narrow, mixture, gain, g_high, g_low)
     later, grad_gain = call(
         suffix_kernel,
         [((count, 2 * rows, DH), f32), ((heads, DH), f32)],
@@ -297,10 +325,13 @@
         cross_scale=cross_scale,
     )(outer)
     later = lax.all_to_all(later, "seq", 0, 0, axis_index_groups=backwards)
+    shapes = [((length, width), bf16)] * 2 + [((src_length, width), bf16)] * 2
     grad_key, grad_value, grad_src_key, grad_src_value = call(
         final_kernel,
-        [((length, width), bf16), ((length, width), bf16), ((src_length, width), bf16), ((src_length, width), bf16)],
+        shapes,
         "final",
+        out_specs=[HBM] * 4,
+        scratch=[pltpu.VMEM(*shape) for shape in shapes] + [pltpu.SemaphoreType.DMA((4,))],
         heads=heads,
         rows=rows,
     )(keys, values, src_keys, src_values, later, grad_key, grad_value)

time: 89 us -> 89.2 us (level)
  Pallas kernels: 9.3 us -> 10.7 us
  local copies, waits for them, and re-layouts: 1.4 us -> 0.04 us
    pallas_call x12, Pallas kernels: 9.3 us -> 10.7 us  [run(): pl.pallas_call(functools.partial(kernel, **static), out_shape=shapes, in_...]
    unnamed x16 -> x14, local copies, waits for them, and re-layouts: 1.4 us -> 0.04 us
  transfers between devices with their start and end apart: 8 -> 8, of which waited for: 3 -> 3; matrix products, arithmetic and copies ran while one was open for 0% -> 0% of each run, Pallas kernels for 7% -> 6%
where the time goes in v6:
time: 89.2 us; the launch traced here: 88.6 us
  starting transfers between devices  47.4 us (53%)
  waiting for transfers between devices  15.4 us (17%)
  blocking collectives  14 us (16%)
  Pallas kernels  10.7 us (12%)
  between operations  0.9 us (1%)
    all_to_all x1, blocking collectives, on_device(): outer = lax.all_to_all(outer, 'seq', 0, 0, axis_index_groups=backwards)  14 us
    all_to_all x1, starting transfers between devices, on_device(): own = lax.all_to_all(own, 'seq', 0, 0)  13.2 us
    pallas_call x12, Pallas kernels, run(): pl.pallas_call(functools.partial(kernel, **static), out_shape=shapes, in_...  10.7 us
    ppermute x3, starting transfers between devices, on_device(): lax.ppermute(held, 'heads', along(d))  9.89 us
    all_to_all x1, waiting for transfers between devices, on_device(): before = lax.all_to_all(before, 'seq', 0, 0).reshape(width, DH)  7.89 us
    all_to_all x1, starting transfers between devices, on_device(): later = lax.all_to_all(later, 'seq', 0, 0, axis_index_groups=backwards)  7.79 us
    all_to_all x1, starting transfers between devices, on_device(): before = lax.all_to_all(before, 'seq', 0, 0).reshape(width, DH)  7.61 us
    ppermute x1, starting transfers between devices, on_device(): across = lax.ppermute(grad_out[None], 'heads', along(4))  6.97 us
  transfers between devices with their start and end apart: 8, of which 3 were waited for; matrix products, arithmetic and copies ran while one was open for 0% of the time, Pallas kernels for 6%

profile of v6, /device:TPU:8, one launch (start us, length us, event | category | flops | bytes accessed | tf_op | source)
XLA Modules:
  0.0 88.6 jit_solution(524998724120632977)
XLA Ops:
  0.6 7.0 %collective-permute-start = (bf16[1,256,256]{2,1,0:T(8,128)(2,1)}, bf16[1,256,256]{2,1,0:T(8,128)(2,1)S(1)}, u32[]{:S(2)}, u32[]{:S(2)}) collective-permute-start(bf16[1,256,256]{2,1,0:T(8,128)(2,1)} %bitcast.7), channel_id=1, source_target_pairs={{0,256},{32,288},{64,320},{96,352},{128,384},{160,416},{192,448},{... | collective-permute-start | bytes 393224 | tf_op jit(solution)/shard_map/ppermute | solution.py:273
  7.6 2.1 %states.1 = f32[32,16,128]{2,1,0:T(8,128)} custom-call(bf16[256,256]{1,0:T(8,128)(2,1)} %k_ref.5, bf16[256,256]{1,0:T(8,128)(2,1)} %v_ref.5, bf16[128,256]{1,0:T(8,128)(2,1)} %sk_ref.1, bf16[128,256]{1,0:T(8,128)(2,1)} %sv_ref.1), custom_call_target="tpu_custom_call" | custom-call | flops 40000000000 | bytes 147600000 | tf_op jit(solution)/shard_map/states/pallas_call | solution.py:222
  9.7 13.2 %all-to-all-start = ((f32[32,16,128]{2,1,0:T(8,128)}), f32[32,16,128]{2,1,0:T(8,128)S(1)}, u32[]{:S(2)}, u32[]{:S(2)}) async-start(f32[32,16,128]{2,1,0:T(8,128)} %states.1), calls=%async_computation | async-start | bytes 524288 | tf_op jit(solution)/shard_map/all_to_all | solution.py:285
  22.9 0.1 pad_add_fusion.place_ref
  23.0 0.3 pack.1
  23.4 0.0 copy-start.1
  23.4 3.4 %collective-permute-start.3 = (bf16[2,256,256]{2,1,0:T(8,128)(2,1)S(1)}, bf16[2,256,256]{2,1,0:T(8,128)(2,1)S(1)}, u32[]{:S(2)}, u32[]{:S(2)}) collective-permute-start(bf16[2,256,256]{2,1,0:T(8,128)(2,1)S(1)} %pack.1), channel_id=1, source_target_pairs={{0,448},{32,96},{64,0},{96,160},{128,64},{160,224},{192,128},{224,... | collective-permute-start | bytes 786440 | tf_op jit(solution)/shard_map/ppermute | solution.py:284
  26.8 2.6 %collective-permute-start.2 = (bf16[2,256,256]{2,1,0:T(8,128)(2,1)S(1)}, bf16[2,256,256]{2,1,0:T(8,128)(2,1)S(1)}, u32[]{:S(2)}, u32[]{:S(2)}) collective-permute-start(bf16[2,256,256]{2,1,0:T(8,128)(2,1)S(1)} %pack.1), channel_id=1, source_target_pairs={{0,64},{32,480},{64,128},{96,32},{128,192},{160,96},{192,256},{224... | collective-permute-start | bytes 786440 | tf_op jit(solution)/shard_map/ppermute | solution.py:284
  29.4 3.9 %collective-permute-start.1 = (bf16[2,256,256]{2,1,0:T(8,128)(2,1)S(1)}, bf16[2,256,256]{2,1,0:T(8,128)(2,1)S(1)}, u32[]{:S(2)}, u32[]{:S(2)}) collective-permute-start(bf16[2,256,256]{2,1,0:T(8,128)(2,1)S(1)} %pack.1), channel_id=1, source_target_pairs={{0,128},{32,416},{64,192},{96,480},{128,256},{160,32},{192,320},{2... | collective-permute-start | bytes 786440 | tf_op jit(solution)/shard_map/ppermute | solution.py:284
  33.3 2.2 %all-to-all-done.in_ref = f32[32,16,128]{2,1,0:T(8,128)S(1)} async-done(((f32[32,16,128]{2,1,0:T(8,128)}), f32[32,16,128]{2,1,0:T(8,128)S(1)}, u32[]{:S(2)}, u32[]{:S(2)}) %all-to-all-start) | async-done | bytes 262176 | tf_op jit(solution)/shard_map/all_to_all | solution.py:285
  35.5 0.7 prefix.1._
  36.2 7.6 %all-to-all-start.1 = ((f32[32,8,128]{2,1,0:T(8,128)}), f32[32,8,128]{2,1,0:T(8,128)S(1)}, u32[]{:S(2)}, u32[]{:S(2)}) async-start(f32[32,8,128]{2,1,0:T(8,128)} %prefix.1._), calls=%async_computation.1 | async-start | bytes 262144 | tf_op jit(solution)/shard_map/all_to_all | solution.py:295
  43.9 0.5 within.1.refs_0_.refs_5_
  44.4 0.1 pad_maximum_fusion.refs_0_
  44.6 1.9 %collective-permute-start.4 = (bf16[8,256,256]{2,1,0:T(8,128)(2,1)S(1)}, bf16[8,256,256]{2,1,0:T(8,128)(2,1)S(1)}, u32[]{:S(2)}, u32[]{:S(2)}) collective-permute-start(bf16[8,256,256]{2,1,0:T(8,128)(2,1)S(1)} %pad_maximum_fusion.refs_0_), channel_id=1, source_target_pairs={{0,32},{32,0},{64,96},{96,64},{128,160},{160,128},{192,224},{224,1... | collective-permute-start | bytes 3145736 | tf_op jit(solution)/shard_map/ppermute | solution.py:294
  46.5 7.9 %all-to-all-done.1 = f32[32,8,128]{2,1,0:T(8,128)S(1)} async-done(((f32[32,8,128]{2,1,0:T(8,128)}), f32[32,8,128]{2,1,0:T(8,128)S(1)}, u32[]{:S(2)}, u32[]{:S(2)}) %all-to-all-start.1) | async-done | bytes 131104 | tf_op jit(solution)/shard_map/all_to_all | solution.py:295
  54.4 3.3 %cotangent.1 = (f32[32,5,2,128]{3,2,1,0:T(2,128)S(1)}, bf16[256,256]{1,0:T(8,128)(2,1)S(1)}, bf16[256,256]{1,0:T(8,128)(2,1)S(1)}, f32[256,256]{1,0:T(8,128)S(1)}) custom-call(s32[2]{0:T(128)S(1)} %pad_add_fusion.place_ref, bf16[8,256,256]{2,1,0:T(8,128)(2,1)S(1)} %pad_maximum_fusion.refs_0_, bf16[8,256,256]{2,1,0:T(8,128)(2,1)S(1)} %collective-permute-done.4.refs_1_, ...), custom_call_target="tpu_custom_call" | custom-call | flops 3000000000 | bytes 11070000 | tf_op jit(solution)/shard_map/cotangent/pallas_call | solution.py:222
  57.7 14.0 %all_to_all.20.in_ref = f32[32,5,2,128]{3,2,1,0:T(2,128)S(1)} all-to-all(f32[32,5,2,128]{3,2,1,0:T(2,128)S(1)} %get-tuple-element.30), channel_id=1, replica_groups={{31,30,29,28,27,26,25,24,23,22,21,20,19,18,17,16,15,14,13,12,11,10,9,8,..., dimensions={0} | all-to-all | bytes 327680 | tf_op jit(solution)/shard_map/all_to_all | solution.py:309
  71.8 0.8 suffix.1
  72.6 7.8 %all-to-all-start.3 = ((f32[32,16,128]{2,1,0:T(8,128)}), f32[32,16,128]{2,1,0:T(8,128)S(1)}, u32[]{:S(2)}, u32[]{:S(2)}) async-start(f32[32,16,128]{2,1,0:T(8,128)} %get-tuple-element.31), calls=%async_computation.3 | async-start | bytes 524288 | tf_op jit(solution)/shard_map/all_to_all | solution.py:327
  80.4 0.0 copy-start.4
  80.4 1.9 %local.1 = (bf16[256,256]{1,0:T(8,128)(2,1)}, bf16[256,256]{1,0:T(8,128)(2,1)}, f32[256,256]{1,0:T(8,128)S(1)}, f32[256,256]{1,0:T(8,128)S(1)}) custom-call(bf16[256,256]{1,0:T(8,128)(2,1)S(1)} %copy-done.1, bf16[256,256]{1,0:T(8,128)(2,1)S(1)} %copy-done.2, bf16[256,256]{1,0:T(8,128)(2,1)S(1)} %copy-done.3, ...), custom_call_target="tpu_custom_call" | custom-call | flops 3000000000 | bytes 11070000 | tf_op jit(solution)/shard_map/local/pallas_call | solution.py:222
  82.3 5.3 %all-to-all-done.3.s_ref = f32[32,16,128]{2,1,0:T(8,128)S(1)} async-done(((f32[32,16,128]{2,1,0:T(8,128)}), f32[32,16,128]{2,1,0:T(8,128)S(1)}, u32[]{:S(2)}, u32[]{:S(2)}) %all-to-all-start.3) | async-done | bytes 262176 | tf_op jit(solution)/shard_map/all_to_all | solution.py:327
  87.6 1.0 %final.1 = (bf16[256,256]{1,0:T(8,128)(2,1)}, bf16[256,256]{1,0:T(8,128)(2,1)}, bf16[128,256]{1,0:T(8,128)(2,1)}, bf16[128,256]{1,0:T(8,128)(2,1)}) custom-call(bf16[256,256]{1,0:T(8,128)(2,1)S(1)} %copy-done.2, bf16[256,256]{1,0:T(8,128)(2,1)S(1)} %copy-done.3, bf16[128,256]{1,0:T(8,128)(2,1)S(1)} %copy-done.4, bf16[128,256]{1,0:T(8,128)(2,1)S(1)} %copy-done.5, ...), custom_call_target="tpu_custom_call" | custom-call | flops 500000000 | bytes 1845000 | tf_op jit(solution)/shard_map/final/pallas_call | solution.py:222
  (21 shorter events, 0.1 us)
Async XLA Ops:
  0.6 22.4 %copy-start = (bf16[256,256]{1,0:T(8,128)(2,1)S(1)}, bf16[256,256]{1,0:T(8,128)(2,1)}, u32[]{:S(2)}) copy-start(bf16[256,256]{1,0:T(8,128)(2,1)} %refs_2_.2) | copy-start | bytes 393220
  0.6 22.4 %collective-permute-start = (bf16[1,256,256]{2,1,0:T(8,128)(2,1)}, bf16[1,256,256]{2,1,0:T(8,128)(2,1)S(1)}, u32[]{:S(2)}, u32[]{:S(2)}) collective-permute-start(bf16[1,256,256]{2,1,0:T(8,128)(2,1)} %bitcast.7), channel_id=1, source_target_pairs={{0,256},{32,288},{64,320},{96,352},{128,384},{160,416},{192,448},{... | collective-permute-start | bytes 393224 | tf_op jit(solution)/shard_map/ppermute | solution.py:273
  9.7 25.8 %all-to-all-start = ((f32[32,16,128]{2,1,0:T(8,128)}), f32[32,16,128]{2,1,0:T(8,128)S(1)}, u32[]{:S(2)}, u32[]{:S(2)}) async-start(f32[32,16,128]{2,1,0:T(8,128)} %states.1), calls=%async_computation | async-start | bytes 524288 | tf_op jit(solution)/shard_map/all_to_all | solution.py:285
  23.4 20.5 %copy-start.1 = (bf16[256,256]{1,0:T(8,128)(2,1)S(1)}, bf16[256,256]{1,0:T(8,128)(2,1)}, u32[]{:S(2)}) copy-start(bf16[256,256]{1,0:T(8,128)(2,1)} %q_ref.3) | copy-start | bytes 393220
  23.4 20.5 %copy-start.2 = (bf16[256,256]{1,0:T(8,128)(2,1)S(1)}, bf16[256,256]{1,0:T(8,128)(2,1)}, u32[]{:S(2)}) copy-start(bf16[256,256]{1,0:T(8,128)(2,1)} %k_ref.5) | copy-start | bytes 393220
  23.4 20.5 %copy-start.3 = (bf16[256,256]{1,0:T(8,128)(2,1)S(1)}, bf16[256,256]{1,0:T(8,128)(2,1)}, u32[]{:S(2)}) copy-start(bf16[256,256]{1,0:T(8,128)(2,1)} %v_ref.5) | copy-start | bytes 393220
  23.4 20.9 %collective-permute-start.3 = (bf16[2,256,256]{2,1,0:T(8,128)(2,1)S(1)}, bf16[2,256,256]{2,1,0:T(8,128)(2,1)S(1)}, u32[]{:S(2)}, u32[]{:S(2)}) collective-permute-start(bf16[2,256,256]{2,1,0:T(8,128)(2,1)S(1)} %pack.1), channel_id=1, source_target_pairs={{0,448},{32,96},{64,0},{96,160},{128,64},{160,224},{192,128},{224,... | collective-permute-start | bytes 786440 | tf_op jit(solution)/shard_map/ppermute | solution.py:284
  26.8 17.6 %collective-permute-start.2 = (bf16[2,256,256]{2,1,0:T(8,128)(2,1)S(1)}, bf16[2,256,256]{2,1,0:T(8,128)(2,1)S(1)}, u32[]{:S(2)}, u32[]{:S(2)}) collective-permute-start(bf16[2,256,256]{2,1,0:T(8,128)(2,1)S(1)} %pack.1), channel_id=1, source_target_pairs={{0,64},{32,480},{64,128},{96,32},{128,192},{160,96},{192,256},{224... | collective-permute-start | bytes 786440 | tf_op jit(solution)/shard_map/ppermute | solution.py:284
  29.4 15.0 %collective-permute-start.1 = (bf16[2,256,256]{2,1,0:T(8,128)(2,1)S(1)}, bf16[2,256,256]{2,1,0:T(8,128)(2,1)S(1)}, u32[]{:S(2)}, u32[]{:S(2)}) collective-permute-start(bf16[2,256,256]{2,1,0:T(8,128)(2,1)S(1)} %pack.1), channel_id=1, source_target_pairs={{0,128},{32,416},{64,192},{96,480},{128,256},{160,32},{192,320},{2... | collective-permute-start | bytes 786440 | tf_op jit(solution)/shard_map/ppermute | solution.py:284
  36.2 18.2 %all-to-all-start.1 = ((f32[32,8,128]{2,1,0:T(8,128)}), f32[32,8,128]{2,1,0:T(8,128)S(1)}, u32[]{:S(2)}, u32[]{:S(2)}) async-start(f32[32,8,128]{2,1,0:T(8,128)} %prefix.1._), calls=%async_computation.1 | async-start | bytes 262144 | tf_op jit(solution)/shard_map/all_to_all | solution.py:295
  44.6 9.8 %collective-permute-start.4 = (bf16[8,256,256]{2,1,0:T(8,128)(2,1)S(1)}, bf16[8,256,256]{2,1,0:T(8,128)(2,1)S(1)}, u32[]{:S(2)}, u32[]{:S(2)}) collective-permute-start(bf16[8,256,256]{2,1,0:T(8,128)(2,1)S(1)} %pad_maximum_fusion.refs_0_), channel_id=1, source_target_pairs={{0,32},{32,0},{64,96},{96,64},{128,160},{160,128},{192,224},{224,1... | collective-permute-start | bytes 3145736 | tf_op jit(solution)/shard_map/ppermute | solution.py:294
  57.7 22.6 %copy-start.6 = (f32[256]{0:T(256)S(1)}, f32[256]{0:T(256)}, u32[]{:S(2)}) copy-start(f32[256]{0:T(256)} %param.13) | copy-start | bytes 3076
  72.6 15.0 %all-to-all-start.3 = ((f32[32,16,128]{2,1,0:T(8,128)}), f32[32,16,128]{2,1,0:T(8,128)S(1)}, u32[]{:S(2)}, u32[]{:S(2)}) async-start(f32[32,16,128]{2,1,0:T(8,128)} %get-tuple-element.31), calls=%async_computation.3 | async-start | bytes 524288 | tf_op jit(solution)/shard_map/all_to_all | solution.py:327
  80.4 7.2 %copy-start.4 = (bf16[128,256]{1,0:T(8,128)(2,1)S(1)}, bf16[128,256]{1,0:T(8,128)(2,1)}, u32[]{:S(2)}) copy-start(bf16[128,256]{1,0:T(8,128)(2,1)} %sk_ref.1) | copy-start | bytes 196612
  80.4 7.2 %copy-start.5 = (bf16[128,256]{1,0:T(8,128)(2,1)S(1)}, bf16[128,256]{1,0:T(8,128)(2,1)}, u32[]{:S(2)}) copy-start(bf16[128,256]{1,0:T(8,128)(2,1)} %sv_ref.1) | copy-start | bytes 196612
